TPU v7x, 512 devices: a whole 4x4x16 slice. The times are simulated.
512 devices in a mesh: ta: 4 (over z_lo), gz: 16 (over z_hi, x), xy: 8 (over y, core).
Axes of the slice: x: 4, y: 4, z: 16 (z_hi: 4, z_lo: 4; z = z_hi * 4 + z_lo), core: 2. Of those that a mesh axis runs over, the one named last changes fastest.
Arguments:
- eigenvectors: bfloat16 [4, 128, 3, 2, 16, 1024], P('ta', ('gz', 'xy')), may hold values from -6 to 6
- gauge_links: bfloat16 [4, 3, 3, 2, 4, 16, 1024], P(None, None, None, None, 'ta', 'gz', 'xy'), may hold values from -2 to 2
- back_links: bfloat16 [4, 3, 3, 2, 4, 16, 1024], P(None, None, None, None, 'ta', 'gz', 'xy'), may hold values from -2 to 2, as said below
- clover: bfloat16 [2, 6, 6, 2, 4, 16, 1024], P(None, None, None, None, 'ta', 'gz', 'xy'), may hold values from -1.25 to 1.25
- source_eigen: int32 [32], replicated, may hold values from 0 to 127
- source_spin: int32 [32], replicated, may hold values from 0 to 3
- source_parity: int32 [32], replicated, may hold values from 0 to 1
Outputs:
- propagated: bfloat16 [32, 4, 3, 2, 4, 16, 1024], P(None, None, None, None, 'ta', 'gz', 'xy')
- projection: float32 [2, 4, 128, 128], P(None, 'ta')
Inputs may be any that keep to these rules, and one draw needn't show every extreme that they name: back_links[d] at each site equals gauge_links[d] at the site one step below along direction d, periodically over the window.
All inputs are finite; a program needn't handle non-finite values.
Results may differ from a plain program's by a relative error of at most 0.0017.
Values may be sent and summed in bfloat16 or wider, within the bound.
No kernel may reach another device: no remote copies, remote signals or barrier semaphores. Data moves between devices by JAX's collectives and lax.ppermute only.
A program may use at most 64 MiB of HBM per device.

v0:
```python
import math

import jax
import jax.numpy as jnp
import numpy as np
from jax import lax
from jax.sharding import PartitionSpec as P

NX = 64


hopping = 0.125


def with_halo(cells, sides, width, closed):
    for axis, dim in sides:
        count = lax.axis_size(axis)
        ends = count if closed else count - 1
        head = lax.slice_in_dim(cells, 0, width, axis=dim)
        tail = lax.slice_in_dim(cells, cells.shape[dim] - width, cells.shape[dim], axis=dim)
        cells = jnp.concatenate(
            [
                lax.ppermute(tail, axis, [(i, (i + 1) % count) for i in range(ends)]),
                cells,
                lax.ppermute(head, axis, [((i + 1) % count, i) for i in range(ends)]),
            ],
            axis=dim,
        )
    return cells


def gamma_parts():
    real_part = np.zeros((4, 4, 4), np.float32)
    imag_part = np.zeros((4, 4, 4), np.float32)
    for direction, row_index, column_index, amount in (
        (0, 0, 3, 1.0),
        (0, 1, 2, 1.0),
        (0, 2, 1, -1.0),
        (0, 3, 0, -1.0),
        (2, 0, 2, 1.0),
        (2, 1, 3, -1.0),
        (2, 2, 0, -1.0),
        (2, 3, 1, 1.0),
    ):
        imag_part[direction, row_index, column_index] = amount
    for direction, row_index, column_index, amount in (
        (1, 0, 3, -1.0),
        (1, 1, 2, 1.0),
        (1, 2, 1, 1.0),
        (1, 3, 0, -1.0),
        (3, 0, 2, 1.0),
        (3, 1, 3, 1.0),
        (3, 2, 0, 1.0),
        (3, 3, 1, 1.0),
    ):
        real_part[direction, row_index, column_index] = amount
    return (real_part, imag_part)


def projectors(factor):
    real_part, imag_part = gamma_parts()
    identity = np.eye(4, dtype=np.float32)[None]
    return (
        jnp.asarray(identity + factor * real_part, jnp.float32),
        jnp.asarray(factor * imag_part, jnp.float32),
    )


def color_apply(link_real, link_imag, values_real, values_imag, adjoint):
    if adjoint:
        link_real = jnp.swapaxes(link_real, 0, 1)
        link_imag = -jnp.swapaxes(link_imag, 0, 1)
    left_real = link_real[None, None]
    left_imag = link_imag[None, None]
    right_real = values_real[:, :, None]
    right_imag = values_imag[:, :, None]
    out_real = jnp.sum(left_real * right_real - left_imag * right_imag, axis=3)
    out_imag = jnp.sum(left_real * right_imag + left_imag * right_real, axis=3)
    return (out_real, out_imag)


def spin_apply(table_real, table_imag, values_real, values_imag):
    trailing = (1,) * (values_real.ndim - 2)
    left_real = table_real.reshape((1, 4, 4) + trailing)
    left_imag = table_imag.reshape((1, 4, 4) + trailing)
    right_real = values_real[:, None]
    right_imag = values_imag[:, None]
    out_real = jnp.sum(left_real * right_real - left_imag * right_imag, axis=2)
    out_imag = jnp.sum(left_real * right_imag + left_imag * right_real, axis=2)
    return (out_real, out_imag)


def clover_apply(clover, values_real, values_imag):
    shape_full = values_real.shape
    blocks_real = values_real.reshape((shape_full[0], 2, 6) + shape_full[3:])
    blocks_imag = values_imag.reshape((shape_full[0], 2, 6) + shape_full[3:])
    clover_real = clover[:, :, :, 0].astype(jnp.float32)[None]
    clover_imag = clover[:, :, :, 1].astype(jnp.float32)[None]
    right_real = blocks_real[:, :, None]
    right_imag = blocks_imag[:, :, None]
    out_real = jnp.sum(clover_real * right_real - clover_imag * right_imag, axis=3)
    out_imag = jnp.sum(clover_real * right_imag + clover_imag * right_real, axis=3)
    return (values_real + out_real.reshape(shape_full), values_imag + out_imag.reshape(shape_full))


def wilson_clover(values_real, values_imag, neighbours, gauge_links, back_links, clover):
    minus_real, minus_imag = projectors(-1.0)
    plus_real, plus_imag = projectors(1.0)
    summed_real, summed_imag = clover_apply(clover, values_real, values_imag)
    for direction in range(4):
        ahead_real, ahead_imag, behind_real, behind_imag = neighbours[direction]
        link_real = gauge_links[direction, :, :, 0].astype(jnp.float32)
        link_imag = gauge_links[direction, :, :, 1].astype(jnp.float32)
        step_real, step_imag = color_apply(link_real, link_imag, ahead_real, ahead_imag, False)
        step_real, step_imag = spin_apply(
            minus_real[direction], minus_imag[direction], step_real, step_imag
        )
        summed_real = summed_real - hopping * step_real
        summed_imag = summed_imag - hopping * step_imag
        link_real = back_links[direction, :, :, 0].astype(jnp.float32)
        link_imag = back_links[direction, :, :, 1].astype(jnp.float32)
        step_real, step_imag = color_apply(link_real, link_imag, behind_real, behind_imag, True)
        step_real, step_imag = spin_apply(
            plus_real[direction], plus_imag[direction], step_real, step_imag
        )
        summed_real = summed_real - hopping * step_real
        summed_imag = summed_imag - hopping * step_imag
    return (summed_real, summed_imag)


def split_parts(segment):
    return (segment[:, :, :, 0].astype(jnp.float32), segment[:, :, :, 1].astype(jnp.float32))


def body(eigenvectors, gauge_links, back_links, clover, source_eigen, source_spin, source_parity):
    time_cells = gauge_links.shape[4]
    depth_cells = gauge_links.shape[5]
    width_cells = NX
    row_cells = gauge_links.shape[6] // width_cells
    plane_cells = row_cells * width_cells
    gauge_links = gauge_links.reshape(gauge_links.shape[:6] + (row_cells, width_cells))
    back_links = back_links.reshape(back_links.shape[:6] + (row_cells, width_cells))
    clover = clover.reshape(clover.shape[:6] + (row_cells, width_cells))
    eigen_local = eigenvectors.shape[1]
    depth_groups = lax.axis_size("gz")
    row_groups = lax.axis_size("xy")
    eigen_count = eigen_local * depth_groups * row_groups
    sources = source_eigen.shape[0]
    pieces = eigenvectors.reshape(
        time_cells, eigen_local, 3, 2, depth_groups, depth_cells, row_groups, plane_cells
    )
    pieces = jnp.transpose(pieces, (4, 6, 0, 1, 2, 3, 5, 7))
    pieces = pieces.reshape(
        depth_groups * row_groups, time_cells, eigen_local, 3, 2, depth_cells, plane_cells
    )
    arrived = lax.all_to_all(pieces, ("gz", "xy"), split_axis=0, concat_axis=0, tiled=True)
    vectors = jnp.transpose(arrived, (1, 0, 2, 3, 4, 5, 6))
    vectors = vectors.reshape(time_cells, eigen_count, 3, 2, depth_cells, row_cells, width_cells)
    grid_shape = (time_cells, depth_cells, row_cells, width_cells)
    parity = (
        lax.broadcasted_iota(jnp.int32, grid_shape, 0)
        + lax.axis_index("ta") * time_cells
        + lax.broadcasted_iota(jnp.int32, grid_shape, 1)
        + lax.axis_index("gz") * depth_cells
        + lax.broadcasted_iota(jnp.int32, grid_shape, 2)
        + lax.axis_index("xy") * row_cells
        + lax.broadcasted_iota(jnp.int32, grid_shape, 3)
    ) % 2
    chosen = jnp.take(vectors, source_eigen, axis=1)
    chosen = jnp.transpose(chosen, (1, 2, 3, 0, 4, 5, 6))
    parity_keep = parity[None] == source_parity[:, None, None, None, None]
    spin_pick = source_spin[:, None] == jnp.arange(4, dtype=jnp.int32)[None]
    condition = (
        spin_pick[:, :, None, None, None, None, None, None] & parity_keep[:, None, None, None]
    )
    source = jnp.where(condition, chosen[:, None], jnp.zeros((), jnp.bfloat16))
    source_real, source_imag = split_parts(source)
    before_after = with_halo(source, (("ta", 4),), 1, False)
    beside_all = with_halo(source, (("gz", 5), ("xy", 6)), 1, True)
    neighbours = [
        split_parts(jnp.roll(source, -1, axis=7)) + split_parts(jnp.roll(source, 1, axis=7)),
        split_parts(beside_all[:, :, :, :, :, 1:-1, 2:])
        + split_parts(beside_all[:, :, :, :, :, 1:-1, :-2]),
        split_parts(beside_all[:, :, :, :, :, 2:, 1:-1])
        + split_parts(beside_all[:, :, :, :, :, :-2, 1:-1]),
        split_parts(before_after[:, :, :, :, 2:]) + split_parts(before_after[:, :, :, :, :-2]),
    ]
    summed_real, summed_imag = wilson_clover(
        source_real, source_imag, neighbours, gauge_links, back_links, clover
    )
    propagated = jnp.stack([summed_real, summed_imag], axis=3).astype(jnp.bfloat16)
    contraction = "teczyx,bactzyx->teab"
    vectors_real = vectors[:, :, :, 0]
    vectors_imag = vectors[:, :, :, 1]
    fields_real = propagated[:, :, :, 0]
    fields_imag = propagated[:, :, :, 1]
    real_sum = jnp.einsum(
        contraction, vectors_real, fields_real, preferred_element_type=jnp.float32
    ) + jnp.einsum(contraction, vectors_imag, fields_imag, preferred_element_type=jnp.float32)
    imag_sum = jnp.einsum(
        contraction, vectors_real, fields_imag, preferred_element_type=jnp.float32
    ) - jnp.einsum(contraction, vectors_imag, fields_real, preferred_element_type=jnp.float32)
    partial_sum = jnp.stack([real_sum, imag_sum]).reshape(2, time_cells, eigen_count, 4 * sources)
    gathered_sum = lax.psum(partial_sum, ("gz", "xy"))
    norm_factor = 1.0 / math.sqrt(
        3.0 * width_cells * row_cells * row_groups * depth_cells * depth_groups
    )
    merged = propagated.reshape(propagated.shape[:6] + (plane_cells,))
    return (merged, gathered_sum * norm_factor)


def solution(mesh):
    placed = (
        P("ta", ("gz", "xy"), None, None, None, None),
        P(None, None, None, None, "ta", "gz", "xy"),
        P(None, None, None, None, "ta", "gz", "xy"),
        P(None, None, None, None, "ta", "gz", "xy"),
        P(),
        P(),
        P(),
    )
    return jax.shard_map(
        body,
        mesh=mesh,
        in_specs=placed,
        out_specs=(P(None, None, None, None, "ta", "gz", "xy"), P(None, "ta", None, None)),
        check_vma=False,
    )
```

profile of v0, /device:TPU:1, one launch (start us, length us, event | category | flops | bytes accessed | tf_op | source)
XLA Modules:
  0.0 1539.6 jit_solution(7096187738157379590)
XLA Ops:
  7.2 1.0 copy.193
  8.2 0.9 copy.161
  9.1 23.0 %all-to-all-start = ((bf16[128,1,1,3,2,1,128]{6,4,3,5,2,1,0:T(2,128)(2,1)}), bf16[128,1,1,3,2,1,128]{6,4,3,5,2,1,0:T(2,128)(2,1)S(1)}, u32[]{:S(2)}, u32[]{:S(2)}) async-start(bf16[128,1,1,3,2,1,128]{6,4,3,5,2,1,0:T(2,128)(2,1)} %copy.161), calls=%async_computation | async-start | bytes 393216 | tf_op jit(solution)/shard_map/all_to_all | solution.py:156
  32.3 0.6 convert_bitcast_fusion.2
  33.0 0.6 negate_bitcast_fusion.2
  34.1 0.6 fusion.39
  34.7 0.7 fusion.33
  35.4 18.0 %all-to-all-done = bf16[128,1,1,3,2,1,128]{6,4,3,5,2,1,0:T(2,128)(2,1)S(1)} async-done(((bf16[128,1,1,3,2,1,128]{6,4,3,5,2,1,0:T(2,128)(2,1)}), bf16[128,1,1,3,2,1,128]{6,4,3,5,2,1,0:T(2,128)(2,1)S(1)}, u32[]{:S(2)}, u32[]{:S(2)}) %all-to-all-start) | async-done | bytes 196640 | tf_op jit(solution)/shard_map/all_to_all | solution.py:156
  53.6 0.6 copy.163
  54.2 0.8 gather_fusion
  55.2 3.7 collective-permute-start.1
  58.9 1.9 collective-permute-start
  61.3 1.3 collective-permute-start.4
  62.6 5.4 collective-permute-start.5
  68.6 1.2 subtract_reduce_fusion.15
  69.8 22.0 %collective-permute-done.1 = bf16[32,4,3,2,1,1,2,64]{7,0,6,2,1,5,4,3:T(8,128)(2,1)S(1)} collective-permute-done((bf16[32,4,3,2,1,1,2,64]{7,0,6,2,1,5,4,3:T(8,128)(2,1)S(1)}, bf16[32,4,3,2,1,1,2,64]{7,0,6,2,1,5,4,3:T(8,128)(2,1)S(1)}, u32[]{:S(2)}, u32[]{:S(2)}) %collective-permute-start.1) | collective-permute-done | bytes 196640 | tf_op jit(solution)/shard_map/ppermute | solution.py:25
  91.8 11.3 collective-permute-done
  103.1 0.3 pad_maximum_fusion
  103.4 0.3 fusion.43
  103.8 0.7 collective-permute-start.2
  104.6 1.1 collective-permute-start.3
  105.8 1.1 fusion.13
  106.9 0.8 add_reduce_fusion.10
  107.9 1.1 fusion.11
  109.0 0.4 add_reduce_fusion.9
  109.5 0.6 copy-done.26
  110.1 0.5 subtract_reduce_fusion.2
  110.8 0.5 subtract_reduce_fusion.1
  111.3 2.1 collective-permute-done.2
  113.4 0.4 fusion.23
  113.8 0.8 add_reduce_fusion.14
  114.8 0.6 copy-done.9
  115.4 1.0 subtract_reduce_fusion.11
  116.5 0.6 copy-done.24
  117.1 0.5 subtract_reduce_fusion.6
  117.8 0.5 subtract_reduce_fusion.5
  118.4 0.3 copy-done
  118.7 0.9 subtract_reduce_fusion
  119.6 3.7 subtract_reduce_fusion.8
  123.3 0.4 fusion.2
  124.0 0.4 fusion.3
  124.5 0.2 convolution_bitcast_fusion
  124.7 0.2 fusion
  125.0 0.2 fusion.1
  125.4 0.7 pad_maximum_fusion.10
  126.7 0.9 copy.186
  127.6 1403.6 %all-reduce.2.cloned.1.call-done = f32[2,1,128,128]{3,2,1,0:T(8,128)} async-done(((f32[2,1,128,128]{3,2,1,0:T(8,128)}), f32[2,1,128,128]{3,2,1,0:T(8,128)}) %all-reduce.2.cloned.1.call-update) | async-done | bytes 131088 | tf_op jit(solution)/shard_map/psum | solution.py:204
  1531.2 1.6 broadcast_multiply_fusion.8
  (100 shorter events, 4.0 us)
Async XLA Ops:
  7.2 25.0 %copy-start.28 = (s32[32]{0:T(128)S(1)}, s32[32]{0:T(128)}, u32[]{:S(2)}) copy-start(s32[32]{0:T(128)} %param.15) | copy-start | bytes 388
  7.2 25.1 %copy-start.16 = (bf16[4,3,3,2,1,1,128]{6,3,5,4,2,1,0:T(2,128)(2,1)S(1)}, bf16[4,3,3,2,1,1,128]{6,3,5,4,2,1,0:T(2,128)(2,1)}, u32[]{:S(2)}) copy-start(bf16[4,3,3,2,1,1,128]{6,3,5,4,2,1,0:T(2,128)(2,1)} %param.13) | copy-start | bytes 55300
  7.2 26.5 %copy-start.29 = (s32[32]{0:T(128)S(1)}, s32[32]{0:T(128)}, u32[]{:S(2)}) copy-start(s32[32]{0:T(128)} %param.16) | copy-start | bytes 388
  7.2 26.5 %copy-start.17 = (bf16[4,3,3,2,1,1,128]{6,3,5,4,2,1,0:T(2,128)(2,1)S(1)}, bf16[4,3,3,2,1,1,128]{6,3,5,4,2,1,0:T(2,128)(2,1)}, u32[]{:S(2)}) copy-start(bf16[4,3,3,2,1,1,128]{6,3,5,4,2,1,0:T(2,128)(2,1)} %param.12) | copy-start | bytes 55300
  7.2 26.6 %copy-start.15 = (bf16[2,6,6,2,1,1,128]{6,3,5,4,2,1,0:T(2,128)(2,1)S(1)}, bf16[2,6,6,2,1,1,128]{6,3,5,4,2,1,0:T(2,128)(2,1)}, u32[]{:S(2)}) copy-start(bf16[2,6,6,2,1,1,128]{6,3,5,4,2,1,0:T(2,128)(2,1)} %param.14) | copy-start | bytes 110596
  7.2 26.7 %copy-start.27 = (s32[32]{0:T(128)S(1)}, s32[32]{0:T(128)}, u32[]{:S(2)}) copy-start(s32[32]{0:T(128)} %param.17) | copy-start | bytes 388
  9.1 44.3 %all-to-all-start = ((bf16[128,1,1,3,2,1,128]{6,4,3,5,2,1,0:T(2,128)(2,1)}), bf16[128,1,1,3,2,1,128]{6,4,3,5,2,1,0:T(2,128)(2,1)S(1)}, u32[]{:S(2)}, u32[]{:S(2)}) async-start(bf16[128,1,1,3,2,1,128]{6,4,3,5,2,1,0:T(2,128)(2,1)} %copy.161), calls=%async_computation | async-start | bytes 393216 | tf_op jit(solution)/shard_map/all_to_all | solution.py:156
  32.1 1499.0 %all-reduce.2.cloned.1.call-start = ((), (), s32[]{:S(2)}) async-start(), calls=%async_computation.1 | async-start | bytes 262144 | tf_op jit(solution)/shard_map/psum | solution.py:204
  55.2 36.6 %collective-permute-start.1 = (bf16[32,4,3,2,1,1,2,64]{7,0,6,2,1,5,4,3:T(8,128)(2,1)S(1)}, bf16[32,4,3,2,1,1,2,64]{7,0,6,2,1,5,4,3:T(8,128)(2,1)S(1)}, u32[]{:S(2)}, u32[]{:S(2)}) collective-permute-start(bf16[32,4,3,2,1,1,2,64]{7,0,6,2,1,5,4,3:T(8,128)(2,1)S(1)} %broadcast_select_fusion), channel_id=1, source_target_pairs={{8,0},{16,8},{24,16},{32,24},{40,32},{48,40},{56,48},{64,56},{72,6... | collective-permute-start | bytes 589832 | tf_op jit(solution)/shard_map/ppermute | solution.py:25
  58.9 44.2 %collective-permute-start = (bf16[32,4,3,2,1,1,2,64]{7,0,6,2,1,5,4,3:T(8,128)(2,1)S(1)}, bf16[32,4,3,2,1,1,2,64]{7,0,6,2,1,5,4,3:T(8,128)(2,1)S(1)}, u32[]{:S(2)}, u32[]{:S(2)}) collective-permute-start(bf16[32,4,3,2,1,1,2,64]{7,0,6,2,1,5,4,3:T(8,128)(2,1)S(1)} %broadcast_select_fusion), channel_id=1, source_target_pairs={{0,8},{8,16},{16,24},{24,32},{32,40},{40,48},{48,56},{56,64},{64,7... | collective-permute-start | bytes 589832 | tf_op jit(solution)/shard_map/ppermute | solution.py:23
  61.3 44.5 %collective-permute-start.4 = (bf16[32,4,3,2,1,1,2,64]{7,0,6,2,1,5,4,3:T(8,128)(2,1)S(1)}, bf16[32,4,3,2,1,1,2,64]{7,0,6,2,1,5,4,3:T(8,128)(2,1)}, u32[]{:S(2)}, u32[]{:S(2)}) collective-permute-start(bf16[32,4,3,2,1,1,2,64]{7,0,6,2,1,5,4,3:T(8,128)(2,1)S(1)} %broadcast_select_fusion), channel_id=1, source_target_pairs={{128,0},{256,128},{384,256},{129,1},{257,129},{385,257},{130,2},{2... | collective-permute-start | bytes 589832 | tf_op jit(solution)/shard_map/ppermute | solution.py:25
  62.6 45.3 %collective-permute-start.5 = (bf16[32,4,3,2,1,1,2,64]{7,0,6,2,1,5,4,3:T(8,128)(2,1)S(1)}, bf16[32,4,3,2,1,1,2,64]{7,0,6,2,1,5,4,3:T(8,128)(2,1)}, u32[]{:S(2)}, u32[]{:S(2)}) collective-permute-start(bf16[32,4,3,2,1,1,2,64]{7,0,6,2,1,5,4,3:T(8,128)(2,1)S(1)} %broadcast_select_fusion), channel_id=1, source_target_pairs={{0,128},{128,256},{256,384},{1,129},{129,257},{257,385},{2,130},{1... | collective-permute-start | bytes 589832 | tf_op jit(solution)/shard_map/ppermute | solution.py:23
  103.8 9.6 collective-permute-start.2
  104.5 2.3 copy-start.5
  104.5 2.3 copy-start.6
  104.5 2.3 copy-start.7
  104.6 2.3 copy-start.8
  104.6 8.8 collective-permute-start.3
  107.8 1.2 copy-start.13
  107.8 1.2 copy-start.14
  109.4 0.7 copy-start.26
  110.1 0.7 copy-start.25
  111.3 2.5 copy-start.2
  111.3 2.5 copy-start.3
  111.3 2.5 copy-start.4
  114.7 0.7 copy-start.9
  114.7 0.7 copy-start.10
  114.7 0.7 copy-start.11
  114.7 0.7 copy-start.12
  116.4 0.7 copy-start.24
  117.1 0.7 copy-start.23
  117.8 0.9 copy-start
  117.8 0.9 copy-start.1
  118.3 1.3 copy-start.18
  118.3 1.3 copy-start.19
  118.3 1.3 copy-start.20
  118.3 1.3 copy-start.21
  118.3 1.3 copy-start.22
Sparse Core Ops, SparseCore 0:
  126.2 1404.9 all-reduce.1
where the time goes:
time: 1540 us
  waiting for transfers between devices  1460 us (95%)
  starting transfers between devices  37.1 us (2%)
  other arithmetic  20.7 us (1%)
    psum x1, waiting for transfers between devices, body(): gathered_sum = lax.psum(partial_sum, ('gz', 'xy'))  1400 us
  transfers between devices with their start and end apart: 8, of which 5 were waited for; matrix products, arithmetic and copies ran while one was open for 1% of the time, Pallas kernels for 0%

commit v1 on v0

v1 whole, which is shorter than its diff:
```python
import math

import jax
import jax.numpy as jnp
from jax import lax
from jax.experimental import pallas as pl
from jax.experimental.pallas import tpu as pltpu
from jax.sharding import Mesh, PartitionSpec as P

hopping = 0.125
SOURCES = 32
EIGEN = 128
SITES = 128
BLOCK = 16


def stencil_kernel(
    vectors_ref,
    center_ref,
    z_up_ref,
    z_down_ref,
    y_up_ref,
    y_down_ref,
    t_up_ref,
    t_down_ref,
    links_ref,
    back_ref,
    clover_ref,
    spin_ref,
    phase_ref,
    out_ref,
    sums_ref,
    rows_ref,
    fields_ref,
    links_f_ref,
    back_f_ref,
    clover_f_ref,
):
    links_f_ref[...] = links_ref[...].astype(jnp.float32)
    back_f_ref[...] = back_ref[...].astype(jnp.float32)
    clover_f_ref[...] = clover_ref[...].astype(jnp.float32)
    lane = lax.broadcasted_iota(jnp.int32, (BLOCK, SITES), 1)
    cell = lane & 63
    first_row = lane < 64
    last_cell = cell == 63
    first_cell = cell == 0
    site_parity = (lane + (lane >> 6)) & 1

    def link(ref, direction, row, column, part):
        index = ((direction * 3 + row) * 3 + column) * 2 + part
        return ref[pl.ds(index, 1), :]

    def forward(direction, real, imag):
        out = []
        for row in range(3):
            re = im = None
            for column in range(3):
                ur = link(links_f_ref, direction, row, column, 0)
                ui = link(links_f_ref, direction, row, column, 1)
                a = ur * real[column] - ui * imag[column]
                b = ur * imag[column] + ui * real[column]
                re = a if re is None else re + a
                im = b if im is None else im + b
            out.append((re, im))
        return out

    def backward(direction, real, imag):
        out = []
        for row in range(3):
            re = im = None
            for column in range(3):
                ur = link(back_f_ref, direction, column, row, 0)
                ui = link(back_f_ref, direction, column, row, 1)
                a = ur * real[column] + ui * imag[column]
                b = ur * imag[column] - ui * real[column]
                re = a if re is None else re + a
                im = b if im is None else im + b
            out.append((re, im))
        return out

    for start in range(0, SOURCES, BLOCK):
        block = pl.ds(start, BLOCK)
        spin = spin_ref[block, :]
        odd = (spin & 1) == 1
        high = spin >= 2
        match = phase_ref[block, :] == site_parity
        sign_x = jnp.where(high, 1.0, -1.0)
        sign_y = jnp.where(odd == high, -1.0, 1.0)

        def load(ref):
            return [ref[k, block, :].astype(jnp.float32) for k in range(6)]

        def both(direction, ahead, behind):
            fwd = forward(direction, ahead[0::2], ahead[1::2])
            bwd = backward(direction, behind[0::2], behind[1::2])
            plus = [(f[0] + b[0], f[1] + b[1]) for f, b in zip(fwd, bwd)]
            minus = [(b[0] - f[0], b[1] - f[1]) for f, b in zip(fwd, bwd)]
            return plus, minus

        center = load(center_ref)
        ahead = [jnp.where(last_cell, pltpu.roll(v, 63, 1), pltpu.roll(v, 127, 1)) for v in center]
        behind = [jnp.where(first_cell, pltpu.roll(v, 65, 1), pltpu.roll(v, 1, 1)) for v in center]
        total, minus = both(0, ahead, behind)
        cross = [(-sign_x * m[1], sign_x * m[0]) for m in minus]
        ahead = [
            pltpu.roll(jnp.where(first_row, n, v), 64, 1) for n, v in zip(load(y_up_ref), center)
        ]
        behind = [
            pltpu.roll(jnp.where(first_row, v, n), 64, 1) for n, v in zip(load(y_down_ref), center)
        ]
        plus, minus = both(1, ahead, behind)
        total = [(s[0] + p[0], s[1] + p[1]) for s, p in zip(total, plus)]
        cross = [(s[0] + sign_y * m[0], s[1] + sign_y * m[1]) for s, m in zip(cross, minus)]
        plus, minus = both(2, load(z_up_ref), load(z_down_ref))
        total = [(s[0] + p[0], s[1] + p[1]) for s, p in zip(total, plus)]
        along = [(-sign_y * m[1], sign_y * m[0]) for m in minus]
        plus, minus = both(3, load(t_up_ref), load(t_down_ref))
        total = [(s[0] + p[0], s[1] + p[1]) for s, p in zip(total, plus)]
        along = [(s[0] + m[0], s[1] + m[1]) for s, m in zip(along, minus)]

        def clover(block_index, row, column, part):
            index = ((block_index * 6 + row) * 6 + column) * 2 + part
            return clover_f_ref[pl.ds(index, 1), :]

        def clover_of(same, row, column, part):
            def one(half, low):
                line = 3 * low + row if same else 3 * (1 - low) + row
                return clover(half, line, 3 * low + column, part)

            lower = jnp.where(odd, one(0, 1), one(0, 0))
            upper = jnp.where(odd, one(1, 1), one(1, 0))
            return jnp.where(high, upper, lower)

        relative = [[], [], [], []]
        for colour in range(3):
            for same in (True, False):
                re = im = None
                for column in range(3):
                    cr = clover_of(same, colour, column, 0)
                    ci = clover_of(same, colour, column, 1)
                    vr, vi = center[2 * column], center[2 * column + 1]
                    a = cr * vr - ci * vi
                    b = cr * vi + ci * vr
                    re = a if re is None else re + a
                    im = b if im is None else im + b
                if same:
                    re = jnp.where(match, center[2 * colour] + re, -hopping * total[colour][0])
                    im = jnp.where(match, center[2 * colour + 1] + im, -hopping * total[colour][1])
                    relative[0] += [re, im]
                else:
                    relative[1] += [jnp.where(match, re, 0.0), jnp.where(match, im, 0.0)]
            relative[2] += [jnp.where(match, 0.0, -hopping * v) for v in along[colour]]
            relative[3] += [jnp.where(match, 0.0, -hopping * v) for v in cross[colour]]
        for k in range(6):
            once = [jnp.where(odd, relative[m ^ 1][k], relative[m][k]) for m in range(4)]
            for b in range(4):
                value = jnp.where(high, once[b ^ 2], once[b])
                rows_ref[pl.ds(start * 24 + b * 6 + k, BLOCK, stride=24), :] = value
                rounded = value.astype(jnp.bfloat16)
                at = pl.ds(b * SOURCES + start, BLOCK)
                fields_ref[at, pl.ds(k * SITES, SITES)] = rounded
                at = pl.ds((4 + b) * SOURCES + start, BLOCK)
                turned = rounded if k % 2 else -rounded
                fields_ref[at, pl.ds((k ^ 1) * SITES, SITES)] = turned
    out_ref[...] = rows_ref[...].astype(jnp.bfloat16)
    product = lax.dot_general(
        vectors_ref[...],
        fields_ref[...],
        (((1,), (1,)), ((), ())),
        preferred_element_type=jnp.float32,
    )
    sums_ref[0] = product[:, : 4 * SOURCES]
    sums_ref[1] = product[:, 4 * SOURCES :]


def apply_stencil(vectors, center, halos, links, back, clover, spin, phase):
    f32 = jnp.float32
    return pl.pallas_call(
        stencil_kernel,
        out_shape=(
            jax.ShapeDtypeStruct((SOURCES * 24, SITES), jnp.bfloat16),
            jax.ShapeDtypeStruct((2, EIGEN, 4 * SOURCES), f32),
        ),
        scratch_shapes=[
            pltpu.VMEM((SOURCES * 24, SITES), f32),
            pltpu.VMEM((8 * SOURCES, 6 * SITES), jnp.bfloat16),
            pltpu.VMEM((72, SITES), f32),
            pltpu.VMEM((72, SITES), f32),
            pltpu.VMEM((144, SITES), f32),
        ],
        compiler_params=pltpu.CompilerParams(vmem_limit_bytes=16 * 2**20),
        cost_estimate=pl.CostEstimate(
            flops=60_000_000, bytes_accessed=1_200_000, transcendentals=0
        ),
        name="stencil",
    )(vectors, center, *halos, links, back, clover, spin, phase)


DOMAIN = ("x", "y", "core")


def ring(count, step, closed=True):
    return [(i, (i + step) % count) for i in range(count) if closed or 0 <= i + step < count]


def body(eigenvectors, gauge_links, back_links, clover, source_eigen, source_spin, source_parity):
    pieces = eigenvectors.reshape(6, 16, 8, SITES).transpose(1, 2, 0, 3).reshape(4, 32, 6, SITES)
    arrived = lax.all_to_all(pieces, "zh", split_axis=0, concat_axis=0, tiled=True)
    arrived = lax.all_to_all(
        arrived.transpose(1, 0, 2, 3), DOMAIN, split_axis=0, concat_axis=0, tiled=True
    )
    vectors = arrived.transpose(1, 0, 2, 3).reshape(EIGEN, 6 * SITES)
    pick = source_eigen[:, None] == jnp.arange(EIGEN, dtype=jnp.int32)[None]
    center = jnp.dot(
        pick.astype(jnp.bfloat16), vectors, preferred_element_type=jnp.float32
    ).astype(jnp.bfloat16)
    center = center.reshape(SOURCES, 6, SITES).transpose(1, 0, 2)
    halos = [
        lax.ppermute(center, ("zh", "x"), ring(16, -1)),
        lax.ppermute(center, ("zh", "x"), ring(16, 1)),
        lax.ppermute(center, ("y", "core"), ring(8, -1)),
        lax.ppermute(center, ("y", "core"), ring(8, 1)),
        lax.ppermute(center, "ta", ring(4, -1, False)),
        lax.ppermute(center, "ta", ring(4, 1, False)),
    ]
    offset = lax.axis_index("ta") + lax.axis_index("x")
    spin = jnp.broadcast_to(source_spin[:, None], (SOURCES, SITES))
    phase = jnp.broadcast_to(((source_parity + offset) & 1)[:, None], (SOURCES, SITES))
    propagated, sums = apply_stencil(
        vectors,
        center,
        halos,
        gauge_links.reshape(72, SITES),
        back_links.reshape(72, SITES),
        clover.reshape(144, SITES),
        spin,
        phase,
    )
    parts = lax.all_to_all(sums.reshape(32, 8, 128), DOMAIN, split_axis=0, concat_axis=0, tiled=True)
    part = jnp.sum(parts, axis=0)
    parts = lax.all_to_all(
        jnp.broadcast_to(part[None], (4, 8, 128)), "zh", split_axis=0, concat_axis=0, tiled=True
    )
    part = jnp.sum(parts, axis=0) * (1.0 / math.sqrt(3.0 * 64 * 16 * 16))
    whole = lax.all_to_all(
        jnp.broadcast_to(part[None], (32, 8, 128)), DOMAIN, split_axis=0, concat_axis=0, tiled=True
    )
    return (
        propagated.reshape(SOURCES, 4, 3, 2, 1, 1, SITES),
        whole.reshape(2, 1, EIGEN, 4 * SOURCES),
    )


def solution(mesh):
    split = Mesh(mesh.devices.reshape(4, 4, 4, 4, 2), ("ta", "zh", "x", "y", "core"))
    fields = P(None, None, None, None, "ta", ("zh", "x"), ("y", "core"))
    return jax.shard_map(
        body,
        mesh=split,
        in_specs=(P("ta", ("zh", "x", "y", "core")), fields, fields, fields, P(), P(), P()),
        out_specs=(fields, P(None, "ta")),
        check_vma=False,
    )
```

time: 1540 us -> 121 us (0.08)
  waiting for transfers between devices: 1460 us -> 1.11 us
  blocking collectives: 0 us -> 95.6 us
  other arithmetic: 20.7 us -> 0.05 us
  starting transfers between devices: 37.1 us -> 17.8 us
    psum x1 -> x0, waiting for transfers between devices: 1400 us -> none  [body(): gathered_sum = lax.psum(partial_sum, ('gz', 'xy'))]
    all_to_all x0 -> x5, blocking collectives: none -> 95.6 us  [the longest x1 28.5 us: body(): lax.all_to_all(pieces, 'zh', split_axis=0, concat_axis=0, tiled=True)]
    ppermute x6, waiting for transfers between devices: 35.4 us -> 1.11 us  [the longest x1 1.1 us: body(): lax.ppermute(center, ('zh', 'x'), ring(16, 1))]
    all_to_all x1 -> x0, starting transfers between devices: 23 us -> none  [body(): lax.all_to_all(pieces, ('gz', 'xy'), split_axis=0, concat_axis=0, tiled=T...]
    all_to_all x1 -> x0, waiting for transfers between devices: 18 us -> none  [body(): lax.all_to_all(pieces, ('gz', 'xy'), split_axis=0, concat_axis=0, tiled=T...]
  transfers between devices with their start and end apart: 8 -> 6, of which waited for: 5 -> 1; matrix products, arithmetic and copies ran while one was open for 1% -> 0% of each run, Pallas kernels for 0% -> 0%
where the time goes in v1:
time: 121 us; the launch traced here: 120 us
  blocking collectives  95.6 us (79%)
  starting transfers between devices  17.8 us (15%)
  local copies, waits for them, and re-layouts  3.28 us (3%)
  Pallas kernels  1.49 us (1%)
    all_to_all x1, blocking collectives, body(): lax.all_to_all(pieces, 'zh', split_axis=0, concat_axis=0, tiled=True)  28.5 us
    all_to_all x1, blocking collectives, body(): lax.all_to_all(arrived.transpose(1, 0, 2, 3), DOMAIN, split_axis=0, conca...  20.1 us
    all_to_all x1, blocking collectives, body(): lax.all_to_all(sums.reshape(32, 8, 128), DOMAIN, split_axis=0, concat_axi...  19.4 us
    all_to_all x1, blocking collectives, body(): lax.all_to_all(jnp.broadcast_to(part[None], (4, 8, 128)), 'zh', split_axi...  14.9 us
    all_to_all x1, blocking collectives, body(): lax.all_to_all(jnp.broadcast_to(part[None], (32, 8, 128)), DOMAIN, split_...  12.7 us
    ppermute x1, starting transfers between devices, body(): lax.ppermute(center, ('zh', 'x'), ring(16, -1))  9.06 us
    ppermute x1, starting transfers between devices, body(): lax.ppermute(center, 'ta', ring(4, 1, False))  4.62 us
    unnamed x15, local copies, waits for them, and re-layouts  2.89 us
  transfers between devices with their start and end apart: 6, of which 1 were waited for; matrix products, arithmetic and copies ran while one was open for 0% of the time, Pallas kernels for 0%

profile of v1, /device:TPU:1, one launch (start us, length us, event | category | flops | bytes accessed | tf_op | source)
XLA Modules:
  0.0 120.3 jit_solution(648590127599277745)
XLA Ops:
  0.6 1.0 copy.29
  1.6 28.5 %all_to_all.25 = bf16[4,32,6,128]{3,1,2,0:T(8,128)(2,1)S(1)} all-to-all(bf16[4,32,6,128]{3,1,2,0:T(8,128)(2,1)S(1)} %copy.23), channel_id=1, replica_groups=mesh['ta'=4,'zh'=4,'x'=4,'y'=4,'core'=2] {'zh'}, dimensions={0} | all-to-all | bytes 393216 | tf_op jit(solution)/shard_map/all_to_all | solution.py:208
  30.1 0.2 copy.24
  30.3 20.1 %all_to_all.26 = bf16[32,4,6,128]{3,1,2,0:T(4,128)(2,1)S(1)} all-to-all(bf16[32,4,6,128]{3,1,2,0:T(4,128)(2,1)S(1)} %copy.24), channel_id=1, replica_groups=mesh['ta'=4,'zh'=4,'x'=4,'y'=4,'core'=2] {'x','y','core'}, dimensions={0} | all-to-all | bytes 393216 | tf_op jit(solution)/shard_map/all_to_all | solution.py:209
  50.3 0.1 copy.25
  50.4 0.0 copy-start.3
  50.4 0.6 copy-done.3
  51.1 0.2 fusion
  51.3 0.0 copy-start.5
  51.3 0.0 copy-start.4
  51.3 0.0 copy-start.2
  51.3 0.0 copy-start
  51.3 4.6 %collective-permute-start.5 = (bf16[6,32,128]{2,1,0:T(8,128)(2,1)S(1)}, bf16[6,32,128]{2,1,0:T(8,128)(2,1)S(1)}, u32[]{:S(2)}, u32[]{:S(2)}) collective-permute-start(bf16[6,32,128]{2,1,0:T(8,128)(2,1)S(1)} %bitcast.35), channel_id=1, source_target_pairs={{0,128},{128,256},{256,384},{1,129},{129,257},{257,385},{2,130},{1... | collective-permute-start | bytes 147464 | tf_op jit(solution)/shard_map/ppermute | solution.py:224
  56.0 1.3 %collective-permute-start.4 = (bf16[6,32,128]{2,1,0:T(8,128)(2,1)S(1)}, bf16[6,32,128]{2,1,0:T(8,128)(2,1)S(1)}, u32[]{:S(2)}, u32[]{:S(2)}) collective-permute-start(bf16[6,32,128]{2,1,0:T(8,128)(2,1)S(1)} %bitcast.36), channel_id=1, source_target_pairs={{128,0},{256,128},{384,256},{129,1},{257,129},{385,257},{130,2},{2... | collective-permute-start | bytes 147464 | tf_op jit(solution)/shard_map/ppermute | solution.py:223
  57.3 0.6 collective-permute-start.3
  57.9 0.0 collective-permute-start.2
  57.9 2.2 %collective-permute-start.1 = (bf16[6,32,128]{2,1,0:T(8,128)(2,1)S(1)}, bf16[6,32,128]{2,1,0:T(8,128)(2,1)S(1)}, u32[]{:S(2)}, u32[]{:S(2)}) collective-permute-start(bf16[6,32,128]{2,1,0:T(8,128)(2,1)S(1)} %bitcast.39), channel_id=1, source_target_pairs={{0,8},{8,16},{16,24},{24,32},{32,40},{40,48},{48,56},{56,64},{64,7... | collective-permute-start | bytes 147464 | tf_op jit(solution)/shard_map/ppermute | solution.py:220
  60.1 0.0 collective-permute-done.5.t_down_ref
  60.1 9.1 %collective-permute-start = (bf16[6,32,128]{2,1,0:T(8,128)(2,1)S(1)}, bf16[6,32,128]{2,1,0:T(8,128)(2,1)S(1)}, u32[]{:S(2)}, u32[]{:S(2)}) collective-permute-start(bf16[6,32,128]{2,1,0:T(8,128)(2,1)S(1)} %bitcast.40), channel_id=1, source_target_pairs={{0,120},{8,0},{16,8},{24,16},{32,24},{40,32},{48,40},{56,48},{64,5... | collective-permute-start | bytes 147464 | tf_op jit(solution)/shard_map/ppermute | solution.py:219
  69.2 0.0 copy-done.5
  69.2 0.0 collective-permute-done.4.t_up_ref
  69.2 0.0 collective-permute-done.3.y_down_ref
  69.2 0.0 collective-permute-done.2.y_up_ref
  69.2 1.1 collective-permute-done.1.z_down_ref
  70.3 0.0 collective-permute-done.z_up_ref
  70.3 0.0 copy-start.1
  70.3 0.1 broadcast_in_dim.9.phase_ref
  70.4 0.0 copy-done.4
  70.4 0.1 broadcast_in_dim.8.spin_ref
  70.5 0.0 copy-done.2
  70.5 0.0 copy-done
  70.5 0.6 copy-done.1
  71.1 1.5 %stencil.1 = (bf16[768,128]{1,0:T(8,128)(2,1)}, f32[2,128,128]{2,1,0:T(8,128)S(1)}) custom-call(bf16[128,768]{1,0:T(8,128)(2,1)S(1)} %bitcast.34, bf16[6,32,128]{2,1,0:T(8,128)(2,1)S(1)} %bitcast.41, bf16[6,32,128]{2,1,0:T(8,128)(2,1)S(1)} %collective-permute-done.z_up_ref, bf16[6,32,128]{2,1,0:T(8,128)(2,1)S(1)} %collective-permute-done.1.z_down_ref, ...), custom_call_target="tpu_custom_call" | custom-call | flops 60000000 | bytes 1200000 | tf_op jit(solution)/shard_map/stencil/pallas_call | solution.py:178
  72.6 19.4 %all_to_all.27 = f32[32,8,128]{2,1,0:T(8,128)S(1)} all-to-all(f32[32,8,128]{2,1,0:T(8,128)S(1)} %bitcast.42), channel_id=1, replica_groups=mesh['ta'=4,'zh'=4,'x'=4,'y'=4,'core'=2] {'x','y','core'}, dimensions={0} | all-to-all | bytes 262144 | tf_op jit(solution)/shard_map/all_to_all | solution.py:239
  92.0 14.9 %all_to_all.28 = f32[4,8,128]{2,1,0:T(8,128)S(1)} all-to-all(f32[4,8,128]{2,1,0:T(8,128)S(1)} %broadcast_in_dim.10), channel_id=1, replica_groups=mesh['ta'=4,'zh'=4,'x'=4,'y'=4,'core'=2] {'zh'}, dimensions={0} | all-to-all | bytes 32768 | tf_op jit(solution)/shard_map/all_to_all | solution.py:241
  106.9 12.7 %all_to_all.29 = f32[32,8,128]{2,1,0:T(8,128)S(1)} all-to-all(f32[32,8,128]{2,1,0:T(8,128)S(1)} %broadcast_in_dim.11), channel_id=1, replica_groups=mesh['ta'=4,'zh'=4,'x'=4,'y'=4,'core'=2] {'x','y','core'}, dimensions={0} | all-to-all | bytes 262144 | tf_op jit(solution)/shard_map/all_to_all | solution.py:245
  119.6 0.7 copy.36
  (9 shorter events, 0.1 us)
Async XLA Ops:
  50.4 0.7 copy-start.3
  51.3 17.9 %copy-start.5 = (s32[32]{0:T(128)S(1)}, s32[32]{0:T(128)}, u32[]{:S(2)}) copy-start(s32[32]{0:T(128)} %param.13) | copy-start | bytes 388
  51.3 19.1 %copy-start.4 = (s32[32]{0:T(128)S(1)}, s32[32]{0:T(128)}, u32[]{:S(2)}) copy-start(s32[32]{0:T(128)} %param.12) | copy-start | bytes 388
  51.3 19.2 %copy-start.2 = (bf16[4,3,3,2,1,1,128]{6,3,5,4,2,1,0:T(2,128)(2,1)S(1)}, bf16[4,3,3,2,1,1,128]{6,3,5,4,2,1,0:T(2,128)(2,1)}, u32[]{:S(2)}) copy-start(bf16[4,3,3,2,1,1,128]{6,3,5,4,2,1,0:T(2,128)(2,1)} %param.9) | copy-start | bytes 55300
  51.3 19.2 %copy-start = (bf16[2,6,6,2,1,1,128]{6,3,5,4,2,1,0:T(2,128)(2,1)S(1)}, bf16[2,6,6,2,1,1,128]{6,3,5,4,2,1,0:T(2,128)(2,1)}, u32[]{:S(2)}) copy-start(bf16[2,6,6,2,1,1,128]{6,3,5,4,2,1,0:T(2,128)(2,1)} %param.10) | copy-start | bytes 110596
  51.3 8.8 %collective-permute-start.5 = (bf16[6,32,128]{2,1,0:T(8,128)(2,1)S(1)}, bf16[6,32,128]{2,1,0:T(8,128)(2,1)S(1)}, u32[]{:S(2)}, u32[]{:S(2)}) collective-permute-start(bf16[6,32,128]{2,1,0:T(8,128)(2,1)S(1)} %bitcast.35), channel_id=1, source_target_pairs={{0,128},{128,256},{256,384},{1,129},{129,257},{257,385},{2,130},{1... | collective-permute-start | bytes 147464 | tf_op jit(solution)/shard_map/ppermute | solution.py:224
  56.0 13.2 %collective-permute-start.4 = (bf16[6,32,128]{2,1,0:T(8,128)(2,1)S(1)}, bf16[6,32,128]{2,1,0:T(8,128)(2,1)S(1)}, u32[]{:S(2)}, u32[]{:S(2)}) collective-permute-start(bf16[6,32,128]{2,1,0:T(8,128)(2,1)S(1)} %bitcast.36), channel_id=1, source_target_pairs={{128,0},{256,128},{384,256},{129,1},{257,129},{385,257},{130,2},{2... | collective-permute-start | bytes 147464 | tf_op jit(solution)/shard_map/ppermute | solution.py:223
  57.3 11.9 %collective-permute-start.3 = (bf16[6,32,128]{2,1,0:T(8,128)(2,1)S(1)}, bf16[6,32,128]{2,1,0:T(8,128)(2,1)S(1)}, u32[]{:S(2)}, u32[]{:S(2)}) collective-permute-start(bf16[6,32,128]{2,1,0:T(8,128)(2,1)S(1)} %bitcast.37), channel_id=1, source_target_pairs={{0,1},{1,2},{2,3},{3,4},{4,5},{5,6},{6,7},{7,0},{8,9},{9,10},{10,1... | collective-permute-start | bytes 147464 | tf_op jit(solution)/shard_map/ppermute | solution.py:222
  57.9 11.4 %collective-permute-start.2 = (bf16[6,32,128]{2,1,0:T(8,128)(2,1)S(1)}, bf16[6,32,128]{2,1,0:T(8,128)(2,1)S(1)}, u32[]{:S(2)}, u32[]{:S(2)}) collective-permute-start(bf16[6,32,128]{2,1,0:T(8,128)(2,1)S(1)} %bitcast.38), channel_id=1, source_target_pairs={{0,7},{1,0},{2,1},{3,2},{4,3},{5,4},{6,5},{7,6},{8,15},{9,8},{10,9... | collective-permute-start | bytes 147464 | tf_op jit(solution)/shard_map/ppermute | solution.py:221
  57.9 12.5 %collective-permute-start.1 = (bf16[6,32,128]{2,1,0:T(8,128)(2,1)S(1)}, bf16[6,32,128]{2,1,0:T(8,128)(2,1)S(1)}, u32[]{:S(2)}, u32[]{:S(2)}) collective-permute-start(bf16[6,32,128]{2,1,0:T(8,128)(2,1)S(1)} %bitcast.39), channel_id=1, source_target_pairs={{0,8},{8,16},{16,24},{24,32},{32,40},{40,48},{48,56},{56,64},{64,7... | collective-permute-start | bytes 147464 | tf_op jit(solution)/shard_map/ppermute | solution.py:220
  60.1 10.2 %collective-permute-start = (bf16[6,32,128]{2,1,0:T(8,128)(2,1)S(1)}, bf16[6,32,128]{2,1,0:T(8,128)(2,1)S(1)}, u32[]{:S(2)}, u32[]{:S(2)}) collective-permute-start(bf16[6,32,128]{2,1,0:T(8,128)(2,1)S(1)} %bitcast.40), channel_id=1, source_target_pairs={{0,120},{8,0},{16,8},{24,16},{32,24},{40,32},{48,40},{56,48},{64,5... | collective-permute-start | bytes 147464 | tf_op jit(solution)/shard_map/ppermute | solution.py:219
  70.3 0.7 copy-start.1

commit v2 on v1

--- a/solution.py
+++ b/solution.py
@@ -17,17 +17,12 @@
 def stencil_kernel(
     vectors_ref,
     center_ref,
-    z_up_ref,
-    z_down_ref,
-    y_up_ref,
-    y_down_ref,
     t_up_ref,
     t_down_ref,
     links_ref,
     back_ref,
     clover_ref,
-    spin_ref,
-    phase_ref,
+    code_ref,
     out_ref,
     sums_ref,
     rows_ref,
@@ -80,15 +75,18 @@
 
     for start in range(0, SOURCES, BLOCK):
         block = pl.ds(start, BLOCK)
-        spin = spin_ref[block, :]
+        code = code_ref[block, :]
+        spin = code >> 3
+        above = (code & 2) != 0
+        below = (code & 4) != 0
         odd = (spin & 1) == 1
         high = spin >= 2
-        match = phase_ref[block, :] == site_parity
+        match = (code & 1) == site_parity
         sign_x = jnp.where(high, 1.0, -1.0)
         sign_y = jnp.where(odd == high, -1.0, 1.0)
 
-        def load(ref):
-            return [ref[k, block, :].astype(jnp.float32) for k in range(6)]
+        def load(ref, first=0):
+            return [ref[first + k, block, :].astype(jnp.float32) for k in range(6)]
 
         def both(direction, ahead, behind):
             fwd = forward(direction, ahead[0::2], ahead[1::2])
@@ -102,19 +100,18 @@
         behind = [jnp.where(first_cell, pltpu.roll(v, 65, 1), pltpu.roll(v, 1, 1)) for v in center]
         total, minus = both(0, ahead, behind)
         cross = [(-sign_x * m[1], sign_x * m[0]) for m in minus]
-        ahead = [
-            pltpu.roll(jnp.where(first_row, n, v), 64, 1) for n, v in zip(load(y_up_ref), center)
-        ]
-        behind = [
-            pltpu.roll(jnp.where(first_row, v, n), 64, 1) for n, v in zip(load(y_down_ref), center)
-        ]
+        beside = load(center_ref, 18)
+        ahead = [pltpu.roll(jnp.where(first_row, n, v), 64, 1) for n, v in zip(beside, center)]
+        behind = [pltpu.roll(jnp.where(first_row, v, n), 64, 1) for n, v in zip(beside, center)]
         plus, minus = both(1, ahead, behind)
         total = [(s[0] + p[0], s[1] + p[1]) for s, p in zip(total, plus)]
         cross = [(s[0] + sign_y * m[0], s[1] + sign_y * m[1]) for s, m in zip(cross, minus)]
-        plus, minus = both(2, load(z_up_ref), load(z_down_ref))
+        plus, minus = both(2, load(center_ref, 12), load(center_ref, 6))
         total = [(s[0] + p[0], s[1] + p[1]) for s, p in zip(total, plus)]
         along = [(-sign_y * m[1], sign_y * m[0]) for m in minus]
-        plus, minus = both(3, load(t_up_ref), load(t_down_ref))
+        ahead = [jnp.where(above, v, 0.0) for v in load(t_up_ref)]
+        behind = [jnp.where(below, v, 0.0) for v in load(t_down_ref)]
+        plus, minus = both(3, ahead, behind)
         total = [(s[0] + p[0], s[1] + p[1]) for s, p in zip(total, plus)]
         along = [(s[0] + m[0], s[1] + m[1]) for s, m in zip(along, minus)]
 
@@ -164,7 +161,7 @@
                 fields_ref[at, pl.ds((k ^ 1) * SITES, SITES)] = turned
     out_ref[...] = rows_ref[...].astype(jnp.bfloat16)
     product = lax.dot_general(
-        vectors_ref[...],
+        vectors_ref[:, : 6 * SITES],
         fields_ref[...],
         (((1,), (1,)), ((), ())),
         preferred_element_type=jnp.float32,
@@ -173,7 +170,7 @@
     sums_ref[1] = product[:, 4 * SOURCES :]
 
 
-def apply_stencil(vectors, center, halos, links, back, clover, spin, phase):
+def apply_stencil(vectors, center, halos, links, back, clover, code):
     f32 = jnp.float32
     return pl.pallas_call(
         stencil_kernel,
@@ -193,7 +190,7 @@
             flops=60_000_000, bytes_accessed=1_200_000, transcendentals=0
         ),
         name="stencil",
-    )(vectors, center, *halos, links, back, clover, spin, phase)
+    )(vectors, center, *halos, links, back, clover, code)
 
 
 DOMAIN = ("x", "y", "core")
@@ -204,28 +201,32 @@
 
 
 def body(eigenvectors, gauge_links, back_links, clover, source_eigen, source_spin, source_parity):
-    pieces = eigenvectors.reshape(6, 16, 8, SITES).transpose(1, 2, 0, 3).reshape(4, 32, 6, SITES)
-    arrived = lax.all_to_all(pieces, "zh", split_axis=0, concat_axis=0, tiled=True)
-    arrived = lax.all_to_all(
-        arrived.transpose(1, 0, 2, 3), DOMAIN, split_axis=0, concat_axis=0, tiled=True
-    )
-    vectors = arrived.transpose(1, 0, 2, 3).reshape(EIGEN, 6 * SITES)
-    pick = source_eigen[:, None] == jnp.arange(EIGEN, dtype=jnp.int32)[None]
+    cells = eigenvectors.reshape(6, 16, 8, SITES).transpose(1, 0, 2, 3)
+    slabs = jnp.stack(
+        [jnp.concatenate([cells[(4 * h - 1) % 16][None], cells[4 * h : 4 * h + 4], cells[(4 * h + 4) % 16][None]]) for h in range(4)]
+    )
+    slabs = lax.all_to_all(slabs, "zh", split_axis=0, concat_axis=0, tiled=True)
+    own = slabs[:, 1:5]
+    first_row = jnp.arange(SITES) < 64
+    beside = jnp.where(first_row, jnp.roll(own, -1, axis=3), jnp.roll(own, 1, axis=3))
+    pieces = jnp.stack([own, slabs[:, :4], slabs[:, 2:], beside])
+    pieces = pieces.transpose(2, 4, 1, 0, 3, 5).reshape(32, 4, 24 * SITES)
+    pieces = lax.all_to_all(pieces, DOMAIN, split_axis=0, concat_axis=0, tiled=True)
+    vectors = pieces.reshape(EIGEN, 24 * SITES)
+    row_of = (source_eigen % 32) * 4 + source_eigen // 32
+    pick = row_of[:, None] == jnp.arange(EIGEN, dtype=jnp.int32)[None]
     center = jnp.dot(
         pick.astype(jnp.bfloat16), vectors, preferred_element_type=jnp.float32
     ).astype(jnp.bfloat16)
-    center = center.reshape(SOURCES, 6, SITES).transpose(1, 0, 2)
+    center = center.reshape(SOURCES, 24, SITES).transpose(1, 0, 2)
     halos = [
-        lax.ppermute(center, ("zh", "x"), ring(16, -1)),
-        lax.ppermute(center, ("zh", "x"), ring(16, 1)),
-        lax.ppermute(center, ("y", "core"), ring(8, -1)),
-        lax.ppermute(center, ("y", "core"), ring(8, 1)),
-        lax.ppermute(center, "ta", ring(4, -1, False)),
-        lax.ppermute(center, "ta", ring(4, 1, False)),
+        lax.ppermute(center[:6], "ta", ring(4, -1, False)),
+        lax.ppermute(center[:6], "ta", ring(4, 1, False)),
     ]
-    offset = lax.axis_index("ta") + lax.axis_index("x")
-    spin = jnp.broadcast_to(source_spin[:, None], (SOURCES, SITES))
-    phase = jnp.broadcast_to(((source_parity + offset) & 1)[:, None], (SOURCES, SITES))
+    time = lax.axis_index("ta")
+    code = (source_parity + time + lax.axis_index("x")) & 1
+    code = code + 2 * (time < 3) + 4 * (time > 0) + 8 * source_spin
+    code = jnp.broadcast_to(code[:, None], (SOURCES, SITES)).astype(jnp.int32)
     propagated, sums = apply_stencil(
         vectors,
         center,
@@ -233,9 +234,9 @@
         gauge_links.reshape(72, SITES),
         back_links.reshape(72, SITES),
         clover.reshape(144, SITES),
-        spin,
-        phase,
-    )
+        code,
+    )
+    sums = sums.reshape(2, 32, 4, 128).transpose(0, 2, 1, 3)
     parts = lax.all_to_all(sums.reshape(32, 8, 128), DOMAIN, split_axis=0, concat_axis=0, tiled=True)
     part = jnp.sum(parts, axis=0)
     parts = lax.all_to_all(

time: 121 us -> 114 us (0.942)
  blocking collectives: 95.6 us -> 40.4 us
  waiting for transfers between devices: 1.11 us -> 28.8 us
  starting transfers between devices: 17.8 us -> 36.2 us
  local copies, waits for them, and re-layouts: 3.28 us -> 4.63 us
    all_to_all x2 -> x0, blocking collectives: 48.6 us -> none  [the longest x1 28.5 us: body(): lax.all_to_all(pieces, 'zh', split_axis=0, concat_axis=0, tiled=True)]
    all_to_all x0 -> x2, starting transfers between devices: none -> 28.4 us  [the longest x1 15.6 us: body(): slabs = lax.all_to_all(slabs, 'zh', split_axis=0, concat_axis=0, tiled=True)]
    all_to_all x0 -> x2, waiting for transfers between devices: none -> 27.7 us  [the longest x1 14.2 us: body(): slabs = lax.all_to_all(slabs, 'zh', split_axis=0, concat_axis=0, tiled=True)]
    ppermute x6 -> x2, starting transfers between devices: 17.8 us -> 7.74 us  [the longest x1 6.45 us: body(): lax.ppermute(center[:6], 'ta', ring(4, 1, False))]
    all_to_all x1, blocking collectives: 19.4 us -> 12.2 us  [body(): lax.all_to_all(sums.reshape(32, 8, 128), DOMAIN, split_axis=0, concat_axi...]
    reshape x2 -> x5, local copies, waits for them, and re-layouts: 0.03 us -> 1.86 us  [the longest x2 1.63 us: body(): pieces = pieces.transpose(2, 4, 1, 0, 3, 5).reshape(32, 4, 24 * SITES)]
    unnamed x15 -> x14, local copies, waits for them, and re-layouts: 2.89 us -> 2.29 us
  transfers between devices with their start and end apart: 6 -> 4, of which waited for: 1 -> 4; matrix products, arithmetic and copies ran while one was open for 0% -> 0% of each run, Pallas kernels for 0% -> 0%
where the time goes in v2:
time: 114 us
  blocking collectives  40.4 us (35%)
  starting transfers between devices  36.2 us (32%)
  waiting for transfers between devices  28.8 us (25%)
  local copies, waits for them, and re-layouts  4.63 us (4%)
  Pallas kernels  1.56 us (1%)
  other arithmetic  1.15 us (1%)
    all_to_all x1, starting transfers between devices, body(): slabs = lax.all_to_all(slabs, 'zh', split_axis=0, concat_axis=0, tiled=True)  15.6 us
    all_to_all x1, blocking collectives, body(): lax.all_to_all(jnp.broadcast_to(part[None], (4, 8, 128)), 'zh', split_axi...  15.5 us
    all_to_all x1, waiting for transfers between devices, body(): slabs = lax.all_to_all(slabs, 'zh', split_axis=0, concat_axis=0, tiled=True)  14.2 us
    all_to_all x1, waiting for transfers between devices, body(): lax.all_to_all(pieces, DOMAIN, split_axis=0, concat_axis=0, tiled=True)  13.5 us
    all_to_all x1, starting transfers between devices, body(): lax.all_to_all(pieces, DOMAIN, split_axis=0, concat_axis=0, tiled=True)  12.8 us
    all_to_all x1, blocking collectives, body(): lax.all_to_all(jnp.broadcast_to(part[None], (32, 8, 128)), DOMAIN, split_...  12.7 us
    all_to_all x1, blocking collectives, body(): lax.all_to_all(sums.reshape(32, 8, 128), DOMAIN, split_axis=0, concat_axi...  12.2 us
    ppermute x1, starting transfers between devices, body(): lax.ppermute(center[:6], 'ta', ring(4, 1, False))  6.45 us
  transfers between devices with their start and end apart: 4, of which 4 were waited for; matrix products, arithmetic and copies ran while one was open for 0% of the time, Pallas kernels for 0%

profile of v2, /device:TPU:1, one launch (start us, length us, event | category | flops | bytes accessed | tf_op | source)
XLA Modules:
  0.0 113.9 jit_solution(11335430664910418885)
XLA Ops:
  0.6 1.0 copy.50
  1.7 0.7 pad_maximum_fusion
  2.5 15.6 %all-to-all-start = ((bf16[4,6,6,8,128]{4,3,2,1,0:T(8,128)(2,1)}), bf16[4,6,6,8,128]{4,3,2,1,0:T(8,128)(2,1)S(1)}, u32[]{:S(2)}, u32[]{:S(2)}) async-start(bf16[4,6,6,8,128]{4,3,2,1,0:T(8,128)(2,1)} %pad_maximum_fusion), calls=%async_computation | async-start | bytes 589824 | tf_op jit(solution)/shard_map/all_to_all | solution.py:208
  18.1 14.2 %all-to-all-done = bf16[4,6,6,8,128]{4,3,2,1,0:T(8,128)(2,1)S(1)} async-done(((bf16[4,6,6,8,128]{4,3,2,1,0:T(8,128)(2,1)}), bf16[4,6,6,8,128]{4,3,2,1,0:T(8,128)(2,1)S(1)}, u32[]{:S(2)}, u32[]{:S(2)}) %all-to-all-start) | async-done | bytes 294944 | tf_op jit(solution)/shard_map/all_to_all | solution.py:208
  32.3 0.1 fusion.4
  32.5 0.1 slice_bitcast_fusion
  32.6 0.2 maximum_select_fusion
  32.8 0.1 slice_bitcast_fusion.4
  32.9 0.1 maximum_bitcast_fusion
  33.0 0.3 copy.47
  33.2 1.4 %reshape.110 = bf16[32,4,3072]{2,1,0:T(4,128)(2,1)} reshape(bf16[4,8,4,4,6,128]{5,4,3,2,1,0:T(8,128)(2,1)S(1)} %copy.47) | data formatting | bytes 1572864 | tf_op jit(solution)/shard_map/reshape | solution.py:213
  34.6 12.8 %all-to-all-start.1 = ((bf16[32,4,3072]{2,1,0:T(4,128)(2,1)}), bf16[32,4,3072]{2,1,0:T(4,128)(2,1)S(1)}, u32[]{:S(2)}, u32[]{:S(2)}) async-start(bf16[32,4,3072]{2,1,0:T(4,128)(2,1)} %reshape.110), calls=%async_computation.1 | async-start | bytes 1572864 | tf_op jit(solution)/shard_map/all_to_all | solution.py:214
  47.4 0.0 copy-start.5
  47.4 0.6 copy-done.5
  48.1 13.5 %all-to-all-done.1 = bf16[32,4,3072]{2,1,0:T(4,128)(2,1)S(1)} async-done(((bf16[32,4,3072]{2,1,0:T(4,128)(2,1)}), bf16[32,4,3072]{2,1,0:T(4,128)(2,1)S(1)}, u32[]{:S(2)}, u32[]{:S(2)}) %all-to-all-start.1) | async-done | bytes 786464 | tf_op jit(solution)/shard_map/all_to_all | solution.py:214
  61.6 0.2 reshape.100.vectors_ref
  61.8 0.3 fusion
  62.1 0.0 copy-start.3
  62.2 0.0 copy-start.4
  62.2 0.0 copy-start
  62.2 0.0 copy-start.2
  62.2 0.0 copy-start.1
  62.2 1.3 %collective-permute-start = (bf16[6,32,128]{2,1,0:T(8,128)(2,1)S(1)}, bf16[6,32,128]{2,1,0:T(8,128)(2,1)S(1)}, u32[]{:S(2)}, u32[]{:S(2)}) collective-permute-start(bf16[6,32,128]{2,1,0:T(8,128)(2,1)S(1)} %slice.88), channel_id=1, source_target_pairs={{128,0},{256,128},{384,256},{129,1},{257,129},{385,257},{130,2},{2... | collective-permute-start | bytes 147464 | tf_op jit(solution)/shard_map/ppermute | solution.py:223
  63.5 6.5 %collective-permute-start.1 = (bf16[6,32,128]{2,1,0:T(8,128)(2,1)S(1)}, bf16[6,32,128]{2,1,0:T(8,128)(2,1)S(1)}, u32[]{:S(2)}, u32[]{:S(2)}) collective-permute-start(bf16[6,32,128]{2,1,0:T(8,128)(2,1)S(1)} %slice.88), channel_id=1, source_target_pairs={{0,128},{128,256},{256,384},{1,129},{129,257},{257,385},{2,130},{1... | collective-permute-start | bytes 147464 | tf_op jit(solution)/shard_map/ppermute | solution.py:224
  70.0 0.0 copy-done.3
  70.0 0.0 copy-done.4
  70.0 0.3 collective-permute-done.t_up_ref
  70.3 0.8 collective-permute-done.1.t_down_ref
  71.1 0.1 broadcast_in_dim.11.code_ref
  71.2 0.0 copy-done
  71.2 0.0 copy-done.2
  71.2 0.0 copy-done.1
  71.2 1.6 %stencil.1 = (bf16[768,128]{1,0:T(8,128)(2,1)}, f32[2,128,128]{2,1,0:T(8,128)S(1)}) custom-call(bf16[128,3072]{1,0:T(8,128)(2,1)S(1)} %reshape.100.vectors_ref, bf16[24,32,128]{2,1,0:T(8,128)(2,1)S(1)} %bitcast.58, bf16[6,32,128]{2,1,0:T(8,128)(2,1)S(1)} %collective-permute-done.t_up_ref, bf16[6,32,128]{2,1,0:T(8,128)(2,1)S(1)} %collective-permute-done.1.t_down_ref, ...), custom_call_target="tpu_custom_call" | custom-call | flops 60000000 | bytes 1200000 | tf_op jit(solution)/shard_map/stencil/pallas_call | solution.py:175
  72.8 12.2 %all_to_all.25 = f32[32,8,128]{2,1,0:T(8,128)S(1)} all-to-all(f32[32,8,128]{2,1,0:T(8,128)S(1)} %bitcast.65), channel_id=1, replica_groups=mesh['ta'=4,'zh'=4,'x'=4,'y'=4,'core'=2] {'x','y','core'}, dimensions={0} | all-to-all | bytes 262144 | tf_op jit(solution)/shard_map/all_to_all | solution.py:240
  85.0 15.5 %all_to_all.26 = f32[4,8,128]{2,1,0:T(8,128)S(1)} all-to-all(f32[4,8,128]{2,1,0:T(8,128)S(1)} %broadcast_in_dim.12), channel_id=1, replica_groups=mesh['ta'=4,'zh'=4,'x'=4,'y'=4,'core'=2] {'zh'}, dimensions={0} | all-to-all | bytes 32768 | tf_op jit(solution)/shard_map/all_to_all | solution.py:242
  100.6 12.7 %all_to_all.27 = f32[32,8,128]{2,1,0:T(8,128)S(1)} all-to-all(f32[32,8,128]{2,1,0:T(8,128)S(1)} %broadcast_in_dim.13), channel_id=1, replica_groups=mesh['ta'=4,'zh'=4,'x'=4,'y'=4,'core'=2] {'x','y','core'}, dimensions={0} | all-to-all | bytes 262144 | tf_op jit(solution)/shard_map/all_to_all | solution.py:246
  113.3 0.7 copy.59
  (20 shorter events, 0.3 us)
Async XLA Ops:
  2.5 29.8 %all-to-all-start = ((bf16[4,6,6,8,128]{4,3,2,1,0:T(8,128)(2,1)}), bf16[4,6,6,8,128]{4,3,2,1,0:T(8,128)(2,1)S(1)}, u32[]{:S(2)}, u32[]{:S(2)}) async-start(bf16[4,6,6,8,128]{4,3,2,1,0:T(8,128)(2,1)} %pad_maximum_fusion), calls=%async_computation | async-start | bytes 589824 | tf_op jit(solution)/shard_map/all_to_all | solution.py:208
  34.6 27.0 %all-to-all-start.1 = ((bf16[32,4,3072]{2,1,0:T(4,128)(2,1)}), bf16[32,4,3072]{2,1,0:T(4,128)(2,1)S(1)}, u32[]{:S(2)}, u32[]{:S(2)}) async-start(bf16[32,4,3072]{2,1,0:T(4,128)(2,1)} %reshape.110), calls=%async_computation.1 | async-start | bytes 1572864 | tf_op jit(solution)/shard_map/all_to_all | solution.py:214
  47.4 0.7 copy-start.5
  62.1 7.8 %copy-start.3 = (s32[32]{0:T(128)S(1)}, s32[32]{0:T(128)}, u32[]{:S(2)}) copy-start(s32[32]{0:T(128)} %param.12) | copy-start | bytes 388
  62.2 7.8 %copy-start.4 = (s32[32]{0:T(128)S(1)}, s32[32]{0:T(128)}, u32[]{:S(2)}) copy-start(s32[32]{0:T(128)} %param.13) | copy-start | bytes 388
  62.2 9.0 %copy-start = (bf16[2,6,6,2,1,1,128]{6,3,5,4,2,1,0:T(2,128)(2,1)S(1)}, bf16[2,6,6,2,1,1,128]{6,3,5,4,2,1,0:T(2,128)(2,1)}, u32[]{:S(2)}) copy-start(bf16[2,6,6,2,1,1,128]{6,3,5,4,2,1,0:T(2,128)(2,1)} %param.10) | copy-start | bytes 110596
  62.2 9.0 %copy-start.2 = (bf16[4,3,3,2,1,1,128]{6,3,5,4,2,1,0:T(2,128)(2,1)S(1)}, bf16[4,3,3,2,1,1,128]{6,3,5,4,2,1,0:T(2,128)(2,1)}, u32[]{:S(2)}) copy-start(bf16[4,3,3,2,1,1,128]{6,3,5,4,2,1,0:T(2,128)(2,1)} %param.9) | copy-start | bytes 55300
  62.2 9.0 %copy-start.1 = (bf16[4,3,3,2,1,1,128]{6,3,5,4,2,1,0:T(2,128)(2,1)S(1)}, bf16[4,3,3,2,1,1,128]{6,3,5,4,2,1,0:T(2,128)(2,1)}, u32[]{:S(2)}) copy-start(bf16[4,3,3,2,1,1,128]{6,3,5,4,2,1,0:T(2,128)(2,1)} %param.8) | copy-start | bytes 55300
  62.2 8.1 %collective-permute-start = (bf16[6,32,128]{2,1,0:T(8,128)(2,1)S(1)}, bf16[6,32,128]{2,1,0:T(8,128)(2,1)S(1)}, u32[]{:S(2)}, u32[]{:S(2)}) collective-permute-start(bf16[6,32,128]{2,1,0:T(8,128)(2,1)S(1)} %slice.88), channel_id=1, source_target_pairs={{128,0},{256,128},{384,256},{129,1},{257,129},{385,257},{130,2},{2... | collective-permute-start | bytes 147464 | tf_op jit(solution)/shard_map/ppermute | solution.py:223
  63.5 7.6 %collective-permute-start.1 = (bf16[6,32,128]{2,1,0:T(8,128)(2,1)S(1)}, bf16[6,32,128]{2,1,0:T(8,128)(2,1)S(1)}, u32[]{:S(2)}, u32[]{:S(2)}) collective-permute-start(bf16[6,32,128]{2,1,0:T(8,128)(2,1)S(1)} %slice.88), channel_id=1, source_target_pairs={{0,128},{128,256},{256,384},{1,129},{129,257},{257,385},{2,130},{1... | collective-permute-start | bytes 147464 | tf_op jit(solution)/shard_map/ppermute | solution.py:224

commit v3 on v2

--- a/solution.py
+++ b/solution.py
@@ -14,9 +14,21 @@
 BLOCK = 16
 
 
+def chosen(pick_ref, vectors_ref, k):
+    return jnp.dot(pick_ref[...], vectors_ref[k], preferred_element_type=jnp.float32)
+
+
+def pick_kernel(pick_ref, vectors_ref, center_ref):
+    for k in range(6):
+        center_ref[k] = chosen(pick_ref, vectors_ref, k).astype(jnp.bfloat16)
+
+
 def stencil_kernel(
     vectors_ref,
+    pick_ref,
     center_ref,
+    y_up_ref,
+    y_down_ref,
     t_up_ref,
     t_down_ref,
     links_ref,
@@ -30,7 +42,10 @@
     links_f_ref,
     back_f_ref,
     clover_f_ref,
+    beside_ref,
 ):
+    for k in range(12):
+        beside_ref[k] = chosen(pick_ref, vectors_ref, 6 + k)
     links_f_ref[...] = links_ref[...].astype(jnp.float32)
     back_f_ref[...] = back_ref[...].astype(jnp.float32)
     clover_f_ref[...] = clover_ref[...].astype(jnp.float32)
@@ -100,13 +115,16 @@
         behind = [jnp.where(first_cell, pltpu.roll(v, 65, 1), pltpu.roll(v, 1, 1)) for v in center]
         total, minus = both(0, ahead, behind)
         cross = [(-sign_x * m[1], sign_x * m[0]) for m in minus]
-        beside = load(center_ref, 18)
-        ahead = [pltpu.roll(jnp.where(first_row, n, v), 64, 1) for n, v in zip(beside, center)]
-        behind = [pltpu.roll(jnp.where(first_row, v, n), 64, 1) for n, v in zip(beside, center)]
+        ahead = [
+            pltpu.roll(jnp.where(first_row, n, v), 64, 1) for n, v in zip(load(y_up_ref), center)
+        ]
+        behind = [
+            pltpu.roll(jnp.where(first_row, v, n), 64, 1) for n, v in zip(load(y_down_ref), center)
+        ]
         plus, minus = both(1, ahead, behind)
         total = [(s[0] + p[0], s[1] + p[1]) for s, p in zip(total, plus)]
         cross = [(s[0] + sign_y * m[0], s[1] + sign_y * m[1]) for s, m in zip(cross, minus)]
-        plus, minus = both(2, load(center_ref, 12), load(center_ref, 6))
+        plus, minus = both(2, load(beside_ref, 6), load(beside_ref))
         total = [(s[0] + p[0], s[1] + p[1]) for s, p in zip(total, plus)]
         along = [(-sign_y * m[1], sign_y * m[0]) for m in minus]
         ahead = [jnp.where(above, v, 0.0) for v in load(t_up_ref)]
@@ -160,17 +178,35 @@
                 turned = rounded if k % 2 else -rounded
                 fields_ref[at, pl.ds((k ^ 1) * SITES, SITES)] = turned
     out_ref[...] = rows_ref[...].astype(jnp.bfloat16)
-    product = lax.dot_general(
-        vectors_ref[:, : 6 * SITES],
-        fields_ref[...],
-        (((1,), (1,)), ((), ())),
-        preferred_element_type=jnp.float32,
-    )
+    product = None
+    for k in range(6):
+        term = lax.dot_general(
+            vectors_ref[k],
+            fields_ref[:, pl.ds(k * SITES, SITES)],
+            (((1,), (1,)), ((), ())),
+            preferred_element_type=jnp.float32,
+        )
+        product = term if product is None else product + term
     sums_ref[0] = product[:, : 4 * SOURCES]
     sums_ref[1] = product[:, 4 * SOURCES :]
 
 
-def apply_stencil(vectors, center, halos, links, back, clover, code):
+def pick_sources(pick, vectors):
+    return pl.pallas_call(
+        pick_kernel,
+        grid=(1,),
+        in_specs=[
+            pl.BlockSpec((SOURCES, EIGEN), lambda i: (0, 0)),
+            pl.BlockSpec((6, EIGEN, SITES), lambda i: (0, 0, 0)),
+        ],
+        out_specs=pl.BlockSpec((6, SOURCES, SITES), lambda i: (0, 0, 0)),
+        out_shape=jax.ShapeDtypeStruct((6, SOURCES, SITES), jnp.bfloat16),
+        compiler_params=pltpu.CompilerParams(vmem_limit_bytes=8 * 2**20),
+        name="pick",
+    )(pick, vectors)
+
+
+def apply_stencil(vectors, pick, center, halos, links, back, clover, code):
     f32 = jnp.float32
     return pl.pallas_call(
         stencil_kernel,
@@ -184,13 +220,14 @@
             pltpu.VMEM((72, SITES), f32),
             pltpu.VMEM((72, SITES), f32),
             pltpu.VMEM((144, SITES), f32),
+            pltpu.VMEM((12, SOURCES, SITES), f32),
         ],
         compiler_params=pltpu.CompilerParams(vmem_limit_bytes=16 * 2**20),
         cost_estimate=pl.CostEstimate(
             flops=60_000_000, bytes_accessed=1_200_000, transcendentals=0
         ),
         name="stencil",
-    )(vectors, center, *halos, links, back, clover, code)
+    )(vectors, pick, center, *halos, links, back, clover, code)
 
 
 DOMAIN = ("x", "y", "core")
@@ -201,41 +238,40 @@
 
 
 def body(eigenvectors, gauge_links, back_links, clover, source_eigen, source_spin, source_parity):
-    cells = eigenvectors.reshape(6, 16, 8, SITES).transpose(1, 0, 2, 3)
-    slabs = jnp.stack(
-        [jnp.concatenate([cells[(4 * h - 1) % 16][None], cells[4 * h : 4 * h + 4], cells[(4 * h + 4) % 16][None]]) for h in range(4)]
-    )
-    slabs = lax.all_to_all(slabs, "zh", split_axis=0, concat_axis=0, tiled=True)
-    own = slabs[:, 1:5]
-    first_row = jnp.arange(SITES) < 64
-    beside = jnp.where(first_row, jnp.roll(own, -1, axis=3), jnp.roll(own, 1, axis=3))
-    pieces = jnp.stack([own, slabs[:, :4], slabs[:, 2:], beside])
-    pieces = pieces.transpose(2, 4, 1, 0, 3, 5).reshape(32, 4, 24 * SITES)
-    pieces = lax.all_to_all(pieces, DOMAIN, split_axis=0, concat_axis=0, tiled=True)
-    vectors = pieces.reshape(EIGEN, 24 * SITES)
-    row_of = (source_eigen % 32) * 4 + source_eigen // 32
-    pick = row_of[:, None] == jnp.arange(EIGEN, dtype=jnp.int32)[None]
-    center = jnp.dot(
-        pick.astype(jnp.bfloat16), vectors, preferred_element_type=jnp.float32
-    ).astype(jnp.bfloat16)
-    center = center.reshape(SOURCES, 24, SITES).transpose(1, 0, 2)
-    halos = [
-        lax.ppermute(center[:6], "ta", ring(4, -1, False)),
-        lax.ppermute(center[:6], "ta", ring(4, 1, False)),
-    ]
     time = lax.axis_index("ta")
     code = (source_parity + time + lax.axis_index("x")) & 1
     code = code + 2 * (time < 3) + 4 * (time > 0) + 8 * source_spin
     code = jnp.broadcast_to(code[:, None], (SOURCES, SITES)).astype(jnp.int32)
-    propagated, sums = apply_stencil(
-        vectors,
-        center,
-        halos,
+    row_of = (source_eigen % 32) * 4 + source_eigen // 32
+    pick = row_of[:, None] == jnp.arange(EIGEN, dtype=jnp.int32)[None]
+    pick = pick.astype(jnp.bfloat16)
+    links, back, clover = (
         gauge_links.reshape(72, SITES),
         back_links.reshape(72, SITES),
         clover.reshape(144, SITES),
-        code,
-    )
+    )
+    cells = eigenvectors.reshape(6, 16, 8, SITES).transpose(1, 0, 2, 3)
+    slabs = jnp.stack(
+        [
+            jnp.concatenate(
+                [cells[(4 * h - 1) % 16][None], cells[4 * h : 4 * h + 4], cells[(4 * h + 4) % 16][None]]
+            )
+            for h in range(4)
+        ]
+    )
+    slabs = lax.all_to_all(slabs, "zh", split_axis=0, concat_axis=0, tiled=True)
+    slabs = slabs.transpose(1, 3, 2, 0, 4).reshape(6, 8, 24, SITES)
+    pieces = jnp.stack([slabs[1:5], slabs[:4], slabs[2:]], axis=2).reshape(32, 72, SITES)
+    pieces = lax.all_to_all(pieces, DOMAIN, split_axis=0, concat_axis=0, tiled=True)
+    vectors = pieces.reshape(32, 18, 4, SITES).transpose(1, 0, 2, 3).reshape(18, EIGEN, SITES)
+    center = pick_sources(pick, vectors)
+    halos = [
+        lax.ppermute(center, ("y", "core"), ring(8, -1)),
+        lax.ppermute(center, ("y", "core"), ring(8, 1)),
+        lax.ppermute(center, "ta", ring(4, -1, False)),
+        lax.ppermute(center, "ta", ring(4, 1, False)),
+    ]
+    propagated, sums = apply_stencil(vectors, pick, center, halos, links, back, clover, code)
     sums = sums.reshape(2, 32, 4, 128).transpose(0, 2, 1, 3)
     parts = lax.all_to_all(sums.reshape(32, 8, 128), DOMAIN, split_axis=0, concat_axis=0, tiled=True)
     part = jnp.sum(parts, axis=0)

time: 114 us -> 112 us (0.982)
  blocking collectives: 40.4 us -> 68.9 us
  waiting for transfers between devices: 28.8 us -> 12.8 us
  starting transfers between devices: 36.2 us -> 22.9 us
    all_to_all x0 -> x1, blocking collectives: none -> 30 us  [body(): slabs = lax.all_to_all(slabs, 'zh', split_axis=0, concat_axis=0, tiled=True)]
    all_to_all x1 -> x0, starting transfers between devices: 15.6 us -> none  [body(): slabs = lax.all_to_all(slabs, 'zh', split_axis=0, concat_axis=0, tiled=True)]
    all_to_all x1 -> x0, waiting for transfers between devices: 14.2 us -> none  [body(): slabs = lax.all_to_all(slabs, 'zh', split_axis=0, concat_axis=0, tiled=True)]
    ppermute x2 -> x4, starting transfers between devices: 7.74 us -> 10.1 us  [the longest x1 7.03 us: body(): lax.ppermute(center, 'ta', ring(4, 1, False))]
    all_to_all x1, waiting for transfers between devices: 13.5 us -> 11.5 us  [body(): lax.all_to_all(pieces, DOMAIN, split_axis=0, concat_axis=0, tiled=True)]
    reshape x4 -> x0, local copies, waits for them, and re-layouts: 1.85 us -> none  [the longest x2 1.63 us: body(): pieces = pieces.transpose(2, 4, 1, 0, 3, 5).reshape(32, 4, 24 * SITES)]
    all_to_all x1, blocking collectives: 15.5 us -> 14.1 us  [body(): lax.all_to_all(jnp.broadcast_to(part[None], (4, 8, 128)), 'zh', split_axi...]
  transfers between devices with their start and end apart: 4 -> 5, of which waited for: 4 -> 3; matrix products, arithmetic and copies ran while one was open for 0% -> 0% of each run, Pallas kernels for 0% -> 0%
where the time goes in v3:
time: 112 us; the launch traced here: 111 us
  blocking collectives  68.9 us (62%)
  starting transfers between devices  22.9 us (20%)
  waiting for transfers between devices  12.8 us (11%)
  local copies, waits for them, and re-layouts  3.89 us (3%)
  Pallas kernels  1.63 us (1%)
    all_to_all x1, blocking collectives, body(): slabs = lax.all_to_all(slabs, 'zh', split_axis=0, concat_axis=0, tiled=True)  30 us
    all_to_all x1, blocking collectives, body(): lax.all_to_all(jnp.broadcast_to(part[None], (4, 8, 128)), 'zh', split_axi...  14.1 us
    all_to_all x1, starting transfers between devices, body(): lax.all_to_all(pieces, DOMAIN, split_axis=0, concat_axis=0, tiled=True)  12.8 us
    all_to_all x1, blocking collectives, body(): lax.all_to_all(jnp.broadcast_to(part[None], (32, 8, 128)), DOMAIN, split_...  12.7 us
    all_to_all x1, blocking collectives, body(): lax.all_to_all(sums.reshape(32, 8, 128), DOMAIN, split_axis=0, concat_axi...  12 us
    all_to_all x1, waiting for transfers between devices, body(): lax.all_to_all(pieces, DOMAIN, split_axis=0, concat_axis=0, tiled=True)  11.5 us
    ppermute x1, starting transfers between devices, body(): lax.ppermute(center, 'ta', ring(4, 1, False))  7.03 us
    unnamed x14, local copies, waits for them, and re-layouts  2.29 us
  transfers between devices with their start and end apart: 5, of which 3 were waited for; matrix products, arithmetic and copies ran while one was open for 0% of the time, Pallas kernels for 0%

profile of v3, /device:TPU:1, one launch (start us, length us, event | category | flops | bytes accessed | tf_op | source)
XLA Modules:
  0.0 111.2 jit_solution(18774163440946151)
XLA Ops:
  0.6 1.0 copy.41
  1.8 30.0 %all_to_all.25 = bf16[4,6,6,8,128]{4,3,2,1,0:T(8,128)(2,1)S(1)} all-to-all(bf16[4,6,6,8,128]{4,3,2,1,0:T(8,128)(2,1)S(1)} %pad_maximum_fusion.1), channel_id=1, replica_groups=mesh['ta'=4,'zh'=4,'x'=4,'y'=4,'core'=2] {'zh'}, dimensions={0} | all-to-all | bytes 589824 | tf_op jit(solution)/shard_map/all_to_all | solution.py:262
  31.8 0.1 copy.44
  31.8 0.1 fusion.3
  31.9 0.1 pad_maximum_fusion
  32.0 0.9 copy.35
  32.9 12.8 %all-to-all-start.1 = ((bf16[32,72,128]{2,1,0:T(8,128)(2,1)}), bf16[32,72,128]{2,1,0:T(8,128)(2,1)S(1)}, u32[]{:S(2)}, u32[]{:S(2)}) async-start(bf16[32,72,128]{2,1,0:T(8,128)(2,1)} %bitcast.9), calls=%async_computation.1 | async-start | bytes 1179648 | tf_op jit(solution)/shard_map/all_to_all | solution.py:265
  45.7 0.0 copy-start.5
  45.7 0.6 copy-done.5
  46.4 0.1 fusion.pick_ref
  46.5 11.5 %all-to-all-done.1 = bf16[32,72,128]{2,1,0:T(8,128)(2,1)S(1)} async-done(((bf16[32,72,128]{2,1,0:T(8,128)(2,1)}), bf16[32,72,128]{2,1,0:T(8,128)(2,1)S(1)}, u32[]{:S(2)}, u32[]{:S(2)}) %all-to-all-start.1) | async-done | bytes 589856 | tf_op jit(solution)/shard_map/all_to_all | solution.py:265
  58.0 0.1 copy.36
  58.1 0.3 copy.37
  58.4 0.0 copy-start.3
  58.4 0.0 copy-start.4
  58.4 0.0 copy-start
  58.4 0.0 copy-start.2
  58.5 0.2 pick.1.center_ref
  58.6 0.0 copy-start.1
  58.6 0.0 collective-permute-start
  58.6 1.7 %collective-permute-start.1 = (bf16[6,32,128]{2,1,0:T(8,128)(2,1)S(1)}, bf16[6,32,128]{2,1,0:T(8,128)(2,1)S(1)}, u32[]{:S(2)}, u32[]{:S(2)}) collective-permute-start(bf16[6,32,128]{2,1,0:T(8,128)(2,1)S(1)} %pick.1.center_ref), channel_id=1, source_target_pairs={{0,1},{1,2},{2,3},{3,4},{4,5},{5,6},{6,7},{7,0},{8,9},{9,10},{10,1... | collective-permute-start | bytes 147464 | tf_op jit(solution)/shard_map/ppermute | solution.py:270
  60.4 1.3 %collective-permute-start.2 = (bf16[6,32,128]{2,1,0:T(8,128)(2,1)S(1)}, bf16[6,32,128]{2,1,0:T(8,128)(2,1)S(1)}, u32[]{:S(2)}, u32[]{:S(2)}) collective-permute-start(bf16[6,32,128]{2,1,0:T(8,128)(2,1)S(1)} %pick.1.center_ref), channel_id=1, source_target_pairs={{128,0},{256,128},{384,256},{129,1},{257,129},{385,257},{130,2},{2... | collective-permute-start | bytes 147464 | tf_op jit(solution)/shard_map/ppermute | solution.py:271
  61.7 7.0 %collective-permute-start.3 = (bf16[6,32,128]{2,1,0:T(8,128)(2,1)S(1)}, bf16[6,32,128]{2,1,0:T(8,128)(2,1)S(1)}, u32[]{:S(2)}, u32[]{:S(2)}) collective-permute-start(bf16[6,32,128]{2,1,0:T(8,128)(2,1)S(1)} %pick.1.center_ref), channel_id=1, source_target_pairs={{0,128},{128,256},{256,384},{1,129},{129,257},{257,385},{2,130},{1... | collective-permute-start | bytes 147464 | tf_op jit(solution)/shard_map/ppermute | solution.py:272
  68.7 0.0 copy-done.3
  68.7 0.0 copy-done.4
  68.7 0.0 collective-permute-done.y_up_ref
  68.8 0.0 collective-permute-done.1.y_down_ref
  68.8 0.1 collective-permute-done.2.t_up_ref
  68.9 1.2 %collective-permute-done.3.t_down_ref = bf16[6,32,128]{2,1,0:T(8,128)(2,1)S(1)} collective-permute-done((bf16[6,32,128]{2,1,0:T(8,128)(2,1)S(1)}, bf16[6,32,128]{2,1,0:T(8,128)(2,1)S(1)}, u32[]{:S(2)}, u32[]{:S(2)}) %collective-permute-start.3) | collective-permute-done | bytes 49184 | tf_op jit(solution)/shard_map/ppermute | solution.py:272
  70.1 0.1 broadcast_in_dim.6.code_ref
  70.1 0.0 copy-done
  70.1 0.0 copy-done.2
  70.1 0.0 copy-done.1
  70.1 1.5 %stencil.1 = (bf16[768,128]{1,0:T(8,128)(2,1)}, f32[2,128,128]{2,1,0:T(8,128)S(1)}) custom-call(bf16[18,128,128]{2,1,0:T(8,128)(2,1)S(1)} %bitcast.42, bf16[32,128]{1,0:T(8,128)(2,1)S(1)} %fusion.pick_ref, bf16[6,32,128]{2,1,0:T(8,128)(2,1)S(1)} %pick.1.center_ref, bf16[6,32,128]{2,1,0:T(8,128)(2,1)S(1)} %collective-permute-done.y_up_ref, ...), custom_call_target="tpu_custom_call" | custom-call | flops 60000000 | bytes 1200000 | tf_op jit(solution)/shard_map/stencil/pallas_call | solution.py:211
  71.6 12.0 %all_to_all.26 = f32[32,8,128]{2,1,0:T(8,128)S(1)} all-to-all(f32[32,8,128]{2,1,0:T(8,128)S(1)} %bitcast.54), channel_id=1, replica_groups=mesh['ta'=4,'zh'=4,'x'=4,'y'=4,'core'=2] {'x','y','core'}, dimensions={0} | all-to-all | bytes 262144 | tf_op jit(solution)/shard_map/all_to_all | solution.py:276
  83.7 14.1 %all_to_all.27 = f32[4,8,128]{2,1,0:T(8,128)S(1)} all-to-all(f32[4,8,128]{2,1,0:T(8,128)S(1)} %broadcast_in_dim.7), channel_id=1, replica_groups=mesh['ta'=4,'zh'=4,'x'=4,'y'=4,'core'=2] {'zh'}, dimensions={0} | all-to-all | bytes 32768 | tf_op jit(solution)/shard_map/all_to_all | solution.py:278
  97.9 12.7 %all_to_all.28 = f32[32,8,128]{2,1,0:T(8,128)S(1)} all-to-all(f32[32,8,128]{2,1,0:T(8,128)S(1)} %broadcast_in_dim.8), channel_id=1, replica_groups=mesh['ta'=4,'zh'=4,'x'=4,'y'=4,'core'=2] {'x','y','core'}, dimensions={0} | all-to-all | bytes 262144 | tf_op jit(solution)/shard_map/all_to_all | solution.py:282
  110.6 0.7 copy.46
  (14 shorter events, 0.2 us)
Async XLA Ops:
  32.9 25.1 %all-to-all-start.1 = ((bf16[32,72,128]{2,1,0:T(8,128)(2,1)}), bf16[32,72,128]{2,1,0:T(8,128)(2,1)S(1)}, u32[]{:S(2)}, u32[]{:S(2)}) async-start(bf16[32,72,128]{2,1,0:T(8,128)(2,1)} %bitcast.9), calls=%async_computation.1 | async-start | bytes 1179648 | tf_op jit(solution)/shard_map/all_to_all | solution.py:265
  45.7 0.7 copy-start.5
  58.4 10.3 %copy-start.3 = (s32[32]{0:T(128)S(1)}, s32[32]{0:T(128)}, u32[]{:S(2)}) copy-start(s32[32]{0:T(128)} %param.12) | copy-start | bytes 388
  58.4 10.3 %copy-start.4 = (s32[32]{0:T(128)S(1)}, s32[32]{0:T(128)}, u32[]{:S(2)}) copy-start(s32[32]{0:T(128)} %param.13) | copy-start | bytes 388
  58.4 11.7 %copy-start = (bf16[2,6,6,2,1,1,128]{6,3,5,4,2,1,0:T(2,128)(2,1)S(1)}, bf16[2,6,6,2,1,1,128]{6,3,5,4,2,1,0:T(2,128)(2,1)}, u32[]{:S(2)}) copy-start(bf16[2,6,6,2,1,1,128]{6,3,5,4,2,1,0:T(2,128)(2,1)} %param.10) | copy-start | bytes 110596
  58.4 11.7 %copy-start.2 = (bf16[4,3,3,2,1,1,128]{6,3,5,4,2,1,0:T(2,128)(2,1)S(1)}, bf16[4,3,3,2,1,1,128]{6,3,5,4,2,1,0:T(2,128)(2,1)}, u32[]{:S(2)}) copy-start(bf16[4,3,3,2,1,1,128]{6,3,5,4,2,1,0:T(2,128)(2,1)} %param.9) | copy-start | bytes 55300
  58.6 11.5 %copy-start.1 = (bf16[4,3,3,2,1,1,128]{6,3,5,4,2,1,0:T(2,128)(2,1)S(1)}, bf16[4,3,3,2,1,1,128]{6,3,5,4,2,1,0:T(2,128)(2,1)}, u32[]{:S(2)}) copy-start(bf16[4,3,3,2,1,1,128]{6,3,5,4,2,1,0:T(2,128)(2,1)} %param.8) | copy-start | bytes 55300
  58.6 10.1 %collective-permute-start = (bf16[6,32,128]{2,1,0:T(8,128)(2,1)S(1)}, bf16[6,32,128]{2,1,0:T(8,128)(2,1)S(1)}, u32[]{:S(2)}, u32[]{:S(2)}) collective-permute-start(bf16[6,32,128]{2,1,0:T(8,128)(2,1)S(1)} %pick.1.center_ref), channel_id=1, source_target_pairs={{0,7},{1,0},{2,1},{3,2},{4,3},{5,4},{6,5},{7,6},{8,15},{9,8},{10,9... | collective-permute-start | bytes 147464 | tf_op jit(solution)/shard_map/ppermute | solution.py:269
  58.6 10.1 %collective-permute-start.1 = (bf16[6,32,128]{2,1,0:T(8,128)(2,1)S(1)}, bf16[6,32,128]{2,1,0:T(8,128)(2,1)S(1)}, u32[]{:S(2)}, u32[]{:S(2)}) collective-permute-start(bf16[6,32,128]{2,1,0:T(8,128)(2,1)S(1)} %pick.1.center_ref), channel_id=1, source_target_pairs={{0,1},{1,2},{2,3},{3,4},{4,5},{5,6},{6,7},{7,0},{8,9},{9,10},{10,1... | collective-permute-start | bytes 147464 | tf_op jit(solution)/shard_map/ppermute | solution.py:270
  60.4 8.5 %collective-permute-start.2 = (bf16[6,32,128]{2,1,0:T(8,128)(2,1)S(1)}, bf16[6,32,128]{2,1,0:T(8,128)(2,1)S(1)}, u32[]{:S(2)}, u32[]{:S(2)}) collective-permute-start(bf16[6,32,128]{2,1,0:T(8,128)(2,1)S(1)} %pick.1.center_ref), channel_id=1, source_target_pairs={{128,0},{256,128},{384,256},{129,1},{257,129},{385,257},{130,2},{2... | collective-permute-start | bytes 147464 | tf_op jit(solution)/shard_map/ppermute | solution.py:271
  61.7 8.4 %collective-permute-start.3 = (bf16[6,32,128]{2,1,0:T(8,128)(2,1)S(1)}, bf16[6,32,128]{2,1,0:T(8,128)(2,1)S(1)}, u32[]{:S(2)}, u32[]{:S(2)}) collective-permute-start(bf16[6,32,128]{2,1,0:T(8,128)(2,1)S(1)} %pick.1.center_ref), channel_id=1, source_target_pairs={{0,128},{128,256},{256,384},{1,129},{129,257},{257,385},{2,130},{1... | collective-permute-start | bytes 147464 | tf_op jit(solution)/shard_map/ppermute | solution.py:272

commit v4 on v3

v4 whole, which is shorter than its diff:
```python
import math

import jax
import jax.numpy as jnp
from jax import lax
from jax.experimental import pallas as pl
from jax.experimental.pallas import tpu as pltpu
from jax.sharding import Mesh, PartitionSpec as P

hopping = 0.125
SOURCES = 32
EIGEN = 128
SITES = 128
BLOCK = 16


def chosen(pick_ref, vectors_ref, k):
    return jnp.dot(pick_ref[...], vectors_ref[k], preferred_element_type=jnp.float32)


def pick_kernel(pick_ref, vectors_ref, code_ref, center_ref, halved_ref):
    lane = lax.broadcasted_iota(jnp.int32, (SOURCES, SITES), 1)
    match = (code_ref[...] & 1) == ((lane + (lane >> 6)) & 1)
    used = []
    for k in range(6):
        value = chosen(pick_ref, vectors_ref, k)
        center_ref[k] = value.astype(jnp.bfloat16)
        used.append(jnp.where(match, value, pltpu.roll(value, 64, 1)))
    for colour in range(3):
        halved_ref[colour] = jnp.where(lane < 64, used[2 * colour], used[2 * colour + 1]).astype(
            jnp.bfloat16
        )


def colour_forward(ref, direction, real, imag):
    out = []
    for row in range(3):
        re = im = None
        for column in range(3):
            index = ((direction * 3 + row) * 3 + column) * 2
            ur, ui = ref[pl.ds(index, 1), :], ref[pl.ds(index + 1, 1), :]
            a = ur * real[column] - ui * imag[column]
            b = ur * imag[column] + ui * real[column]
            re = a if re is None else re + a
            im = b if im is None else im + b
        out.append((re, im))
    return out


def colour_backward(ref, direction, real, imag):
    out = []
    for row in range(3):
        re = im = None
        for column in range(3):
            index = ((direction * 3 + column) * 3 + row) * 2
            ur, ui = ref[pl.ds(index, 1), :], ref[pl.ds(index + 1, 1), :]
            a = ur * real[column] + ui * imag[column]
            b = ur * imag[column] - ui * real[column]
            re = a if re is None else re + a
            im = b if im is None else im + b
        out.append((re, im))
    return out


def both(links_ref, back_ref, direction, ahead, behind):
    fwd = colour_forward(links_ref, direction, ahead[0::2], ahead[1::2])
    bwd = colour_backward(back_ref, direction, behind[0::2], behind[1::2])
    plus = [(f[0] + b[0], f[1] + b[1]) for f, b in zip(fwd, bwd)]
    minus = [(b[0] - f[0], b[1] - f[1]) for f, b in zip(fwd, bwd)]
    return plus, minus


def space_kernel(
    others_ref,
    pick_ref,
    center_ref,
    y_up_ref,
    y_down_ref,
    links_ref,
    back_ref,
    clover_ref,
    code_ref,
    base_ref,
    links_f_ref,
    back_f_ref,
    clover_f_ref,
    beside_ref,
):
    for k in range(12):
        beside_ref[k] = chosen(pick_ref, others_ref, k)
    links_f_ref[...] = links_ref[...].astype(jnp.float32)
    back_f_ref[...] = back_ref[...].astype(jnp.float32)
    clover_f_ref[...] = clover_ref[...].astype(jnp.float32)
    lane = lax.broadcasted_iota(jnp.int32, (BLOCK, SITES), 1)
    cell = lane & 63
    first_row = lane < 64
    last_cell = cell == 63
    first_cell = cell == 0
    site_parity = (lane + (lane >> 6)) & 1

    for start in range(0, SOURCES, BLOCK):
        block = pl.ds(start, BLOCK)
        code = code_ref[block, :]
        spin = code >> 3
        odd = (spin & 1) == 1
        high = spin >= 2
        match = (code & 1) == site_parity
        sign_x = jnp.where(high, 1.0, -1.0)
        sign_y = jnp.where(odd == high, -1.0, 1.0)

        def load(ref, first=0):
            return [ref[first + k, block, :].astype(jnp.float32) for k in range(6)]

        center = load(center_ref)
        ahead = [jnp.where(last_cell, pltpu.roll(v, 63, 1), pltpu.roll(v, 127, 1)) for v in center]
        behind = [jnp.where(first_cell, pltpu.roll(v, 65, 1), pltpu.roll(v, 1, 1)) for v in center]
        total, minus = both(links_f_ref, back_f_ref, 0, ahead, behind)
        cross = [(-sign_x * m[1], sign_x * m[0]) for m in minus]
        ahead = [
            pltpu.roll(jnp.where(first_row, n, v), 64, 1) for n, v in zip(load(y_up_ref), center)
        ]
        behind = [
            pltpu.roll(jnp.where(first_row, v, n), 64, 1) for n, v in zip(load(y_down_ref), center)
        ]
        plus, minus = both(links_f_ref, back_f_ref, 1, ahead, behind)
        total = [(s[0] + p[0], s[1] + p[1]) for s, p in zip(total, plus)]
        cross = [(s[0] + sign_y * m[0], s[1] + sign_y * m[1]) for s, m in zip(cross, minus)]
        plus, minus = both(links_f_ref, back_f_ref, 2, load(beside_ref, 6), load(beside_ref))
        total = [(s[0] + p[0], s[1] + p[1]) for s, p in zip(total, plus)]
        along = [(-sign_y * m[1], sign_y * m[0]) for m in minus]
        def clover(block_index, row, column, part):
            index = ((block_index * 6 + row) * 6 + column) * 2 + part
            return clover_f_ref[pl.ds(index, 1), :]

        def clover_of(same, row, column, part):
            def one(half, low):
                line = 3 * low + row if same else 3 * (1 - low) + row
                return clover(half, line, 3 * low + column, part)

            lower = jnp.where(odd, one(0, 1), one(0, 0))
            upper = jnp.where(odd, one(1, 1), one(1, 0))
            return jnp.where(high, upper, lower)

        relative = [[], [], [], []]
        for colour in range(3):
            for same in (True, False):
                re = im = None
                for column in range(3):
                    cr = clover_of(same, colour, column, 0)
                    ci = clover_of(same, colour, column, 1)
                    vr, vi = center[2 * column], center[2 * column + 1]
                    a = cr * vr - ci * vi
                    b = cr * vi + ci * vr
                    re = a if re is None else re + a
                    im = b if im is None else im + b
                if same:
                    re = jnp.where(match, center[2 * colour] + re, -hopping * total[colour][0])
                    im = jnp.where(match, center[2 * colour + 1] + im, -hopping * total[colour][1])
                    relative[0] += [re, im]
                else:
                    relative[1] += [jnp.where(match, re, 0.0), jnp.where(match, im, 0.0)]
            relative[2] += [jnp.where(match, 0.0, -hopping * v) for v in along[colour]]
            relative[3] += [jnp.where(match, 0.0, -hopping * v) for v in cross[colour]]
        for m in range(4):
            for k in range(6):
                base_ref[6 * m + k, block, :] = relative[m][k]


def spread(ref, block, there, first_row):
    out = []
    for colour in range(3):
        value = jnp.where(there, ref[colour, block, :].astype(jnp.float32), 0.0)
        turned = pltpu.roll(value, 64, 1)
        out += [jnp.where(first_row, value, turned), jnp.where(first_row, turned, value)]
    return out


def time_kernel(
    vectors_ref,
    base_ref,
    t_up_ref,
    t_down_ref,
    links_ref,
    back_ref,
    code_ref,
    out_ref,
    sums_ref,
    rows_ref,
    fields_ref,
    links_f_ref,
    back_f_ref,
):
    links_f_ref[...] = links_ref[...].astype(jnp.float32)
    back_f_ref[...] = back_ref[...].astype(jnp.float32)
    lane = lax.broadcasted_iota(jnp.int32, (BLOCK, SITES), 1)
    first_row = lane < 64
    site_parity = (lane + (lane >> 6)) & 1
    for start in range(0, SOURCES, BLOCK):
        block = pl.ds(start, BLOCK)
        code = code_ref[block, :]
        spin = code >> 3
        above = (code & 2) != 0
        below = (code & 4) != 0
        odd = (spin & 1) == 1
        high = spin >= 2
        match = (code & 1) == site_parity
        ahead = spread(t_up_ref, block, above, first_row)
        behind = spread(t_down_ref, block, below, first_row)
        plus, minus = both(links_f_ref, back_f_ref, 3, ahead, behind)
        relative = [[base_ref[6 * m + k, block, :] for k in range(6)] for m in range(4)]
        for colour in range(3):
            for part in range(2):
                k = 2 * colour + part
                relative[0][k] += jnp.where(match, 0.0, -hopping * plus[colour][part])
                relative[2][k] += jnp.where(match, 0.0, -hopping * minus[colour][part])
        for k in range(6):
            once = [jnp.where(odd, relative[m ^ 1][k], relative[m][k]) for m in range(4)]
            for b in range(4):
                value = jnp.where(high, once[b ^ 2], once[b])
                rows_ref[pl.ds(start * 24 + b * 6 + k, BLOCK, stride=24), :] = value
                rounded = value.astype(jnp.bfloat16)
                at = pl.ds(b * SOURCES + start, BLOCK)
                fields_ref[at, pl.ds(k * SITES, SITES)] = rounded
                at = pl.ds((4 + b) * SOURCES + start, BLOCK)
                turned = rounded if k % 2 else -rounded
                fields_ref[at, pl.ds((k ^ 1) * SITES, SITES)] = turned
    out_ref[...] = rows_ref[...].astype(jnp.bfloat16)
    product = None
    for k in range(6):
        term = lax.dot_general(
            vectors_ref[k],
            fields_ref[:, pl.ds(k * SITES, SITES)],
            (((1,), (1,)), ((), ())),
            preferred_element_type=jnp.float32,
        )
        product = term if product is None else product + term
    sums_ref[0] = product[:, : 4 * SOURCES]
    sums_ref[1] = product[:, 4 * SOURCES :]


def pick_sources(pick, vectors, code):
    return pl.pallas_call(
        pick_kernel,
        out_shape=(
            jax.ShapeDtypeStruct((6, SOURCES, SITES), jnp.bfloat16),
            jax.ShapeDtypeStruct((3, SOURCES, SITES), jnp.bfloat16),
        ),
        compiler_params=pltpu.CompilerParams(vmem_limit_bytes=8 * 2**20),
        name="pick",
    )(pick, vectors, code)


def space_part(others, pick, center, y_up, y_down, links, back, clover, code):
    f32 = jnp.float32
    return pl.pallas_call(
        space_kernel,
        out_shape=jax.ShapeDtypeStruct((24, SOURCES, SITES), f32),
        scratch_shapes=[
            pltpu.VMEM((72, SITES), f32),
            pltpu.VMEM((72, SITES), f32),
            pltpu.VMEM((144, SITES), f32),
            pltpu.VMEM((12, SOURCES, SITES), f32),
        ],
        compiler_params=pltpu.CompilerParams(vmem_limit_bytes=16 * 2**20),
        cost_estimate=pl.CostEstimate(
            flops=20_000_000, bytes_accessed=1_200_000, transcendentals=0
        ),
        name="space",
    )(others, pick, center, y_up, y_down, links, back, clover, code)


def time_part(vectors, base, t_up, t_down, links, back, code):
    f32 = jnp.float32
    return pl.pallas_call(
        time_kernel,
        out_shape=(
            jax.ShapeDtypeStruct((SOURCES * 24, SITES), jnp.bfloat16),
            jax.ShapeDtypeStruct((2, EIGEN, 4 * SOURCES), f32),
        ),
        scratch_shapes=[
            pltpu.VMEM((SOURCES * 24, SITES), f32),
            pltpu.VMEM((8 * SOURCES, 6 * SITES), jnp.bfloat16),
            pltpu.VMEM((72, SITES), f32),
            pltpu.VMEM((72, SITES), f32),
        ],
        compiler_params=pltpu.CompilerParams(vmem_limit_bytes=16 * 2**20),
        cost_estimate=pl.CostEstimate(
            flops=60_000_000, bytes_accessed=1_200_000, transcendentals=0
        ),
        name="time",
    )(vectors, base, t_up, t_down, links, back, code)


DOMAIN = ("x", "y", "core")


def ring(count, step, closed=True):
    return [(i, (i + step) % count) for i in range(count) if closed or 0 <= i + step < count]


def body(eigenvectors, gauge_links, back_links, clover, source_eigen, source_spin, source_parity):
    time = lax.axis_index("ta")
    offset = (time + lax.axis_index("x")) & 1
    ends = 2 * (time < 3).astype(jnp.int32) + 4 * (time > 0).astype(jnp.int32)
    eigenvectors, offset, ends = lax.optimization_barrier((eigenvectors, offset, ends))
    code = ((source_parity + offset) & 1) + ends + 8 * source_spin
    code = jnp.broadcast_to(code[:, None], (SOURCES, SITES)).astype(jnp.int32)
    row_of = (source_eigen % 32) * 4 + source_eigen // 32
    pick = row_of[:, None] == jnp.arange(EIGEN, dtype=jnp.int32)[None]
    pick = pick.astype(jnp.bfloat16)
    links, back, clover = (
        gauge_links.reshape(72, SITES),
        back_links.reshape(72, SITES),
        clover.reshape(144, SITES),
    )
    cells = eigenvectors.reshape(6, 16, 8, SITES).transpose(1, 0, 2, 3)
    slabs = jnp.stack(
        [
            jnp.concatenate(
                [cells[(4 * h - 1) % 16][None], cells[4 * h : 4 * h + 4], cells[(4 * h + 4) % 16][None]]
            )
            for h in range(4)
        ]
    )
    slabs = lax.all_to_all(slabs, "zh", split_axis=0, concat_axis=0, tiled=True)
    slabs = slabs.transpose(1, 3, 2, 0, 4).reshape(6, 8, 24, SITES)
    pieces = jnp.stack([slabs[1:5], slabs[:4], slabs[2:]], axis=2).reshape(32, 72, SITES)
    pieces = lax.all_to_all(pieces, DOMAIN, split_axis=0, concat_axis=0, tiled=True)
    pieces = pieces.reshape(32, 18, 4, SITES)
    vectors = pieces[:, :6].transpose(1, 0, 2, 3).reshape(6, EIGEN, SITES)
    others = pieces[:, 6:].transpose(1, 0, 2, 3).reshape(12, EIGEN, SITES)
    center, halved = pick_sources(pick, vectors, code)
    halos = [
        lax.ppermute(center, ("y", "core"), ring(8, -1)),
        lax.ppermute(center, ("y", "core"), ring(8, 1)),
        lax.ppermute(halved, "ta", ring(4, -1, False)),
        lax.ppermute(halved, "ta", ring(4, 1, False)),
    ]
    base = space_part(others, pick, center, halos[0], halos[1], links, back, clover, code)
    propagated, sums = time_part(vectors, base, halos[2], halos[3], links, back, code)
    sums = sums.reshape(2, 32, 4, 128).transpose(0, 2, 1, 3)
    parts = sums.reshape(8, 4, 8, 128).transpose(1, 0, 2, 3).reshape(32, 8, 128)
    parts = lax.all_to_all(parts, DOMAIN, split_axis=0, concat_axis=0, tiled=True)
    part = jnp.sum(parts, axis=0)
    parts = lax.all_to_all(
        jnp.broadcast_to(part[None], (16, 8, 128)), ("zh", "x"), split_axis=0, concat_axis=0, tiled=True
    )
    part = jnp.sum(parts.reshape(4, 32, 128), axis=0) * (1.0 / math.sqrt(3.0 * 64 * 16 * 16))
    whole = lax.all_to_all(
        jnp.broadcast_to(part[None], (8, 32, 128)), ("y", "core"), split_axis=0, concat_axis=0, tiled=True
    )
    return (
        propagated.reshape(SOURCES, 4, 3, 2, 1, 1, SITES),
        whole.reshape(2, 1, EIGEN, 4 * SOURCES),
    )


def solution(mesh):
    split = Mesh(mesh.devices.reshape(4, 4, 4, 4, 2), ("ta", "zh", "x", "y", "core"))
    fields = P(None, None, None, None, "ta", ("zh", "x"), ("y", "core"))
    return jax.shard_map(
        body,
        mesh=split,
        in_specs=(P("ta", ("zh", "x", "y", "core")), fields, fields, fields, P(), P(), P()),
        out_specs=(fields, P(None, "ta")),
        check_vma=False,
    )
```

time: 112 us -> 111 us (level)
  waiting for transfers between devices: 12.8 us -> 11.5 us
    ppermute x2, waiting for transfers between devices: 1.29 us -> 0.01 us  [the longest x1 0.01 us: body(): lax.ppermute(halved, 'ta', ring(4, -1, False))]
  transfers between devices with their start and end apart: 5 -> 5, of which waited for: 3 -> 1; matrix products, arithmetic and copies ran while one was open for 0% -> 0% of each run, Pallas kernels for 0% -> 1%
where the time goes in v4:
time: 111 us
  blocking collectives  69 us (62%)
  starting transfers between devices  23 us (21%)
  waiting for transfers between devices  11.5 us (10%)
  local copies, waits for them, and re-layouts  4.45 us (4%)
  Pallas kernels  1.78 us (2%)
    all_to_all x1, blocking collectives, body(): slabs = lax.all_to_all(slabs, 'zh', split_axis=0, concat_axis=0, tiled=True)  30 us
    all_to_all x1, blocking collectives, body(): lax.all_to_all(jnp.broadcast_to(part[None], (16, 8, 128)), ('zh', 'x'), s...  17.3 us
    all_to_all x1, starting transfers between devices, body(): lax.all_to_all(pieces, DOMAIN, split_axis=0, concat_axis=0, tiled=True)  12.9 us
    all_to_all x1, blocking collectives, body(): lax.all_to_all(parts, DOMAIN, split_axis=0, concat_axis=0, tiled=True)  12.2 us
    all_to_all x1, waiting for transfers between devices, body(): lax.all_to_all(pieces, DOMAIN, split_axis=0, concat_axis=0, tiled=True)  11.5 us
    all_to_all x1, blocking collectives, body(): lax.all_to_all(jnp.broadcast_to(part[None], (8, 32, 128)), ('y', 'core'),...  9.47 us
    ppermute x1, starting transfers between devices, body(): lax.ppermute(halved, 'ta', ring(4, 1, False))  7.03 us
    unnamed x14, local copies, waits for them, and re-layouts  2.8 us
  transfers between devices with their start and end apart: 5, of which 1 were waited for; matrix products, arithmetic and copies ran while one was open for 0% of the time, Pallas kernels for 1%

profile of v4, /device:TPU:1, one launch (start us, length us, event | category | flops | bytes accessed | tf_op | source)
XLA Modules:
  0.0 110.9 jit_solution(9452670595176786075)
XLA Ops:
  0.6 1.0 copy.49
  1.8 30.0 %all_to_all.25 = bf16[4,6,6,8,128]{4,3,2,1,0:T(8,128)(2,1)S(1)} all-to-all(bf16[4,6,6,8,128]{4,3,2,1,0:T(8,128)(2,1)S(1)} %pad_maximum_fusion.1), channel_id=1, replica_groups=mesh['ta'=4,'zh'=4,'x'=4,'y'=4,'core'=2] {'zh'}, dimensions={0} | all-to-all | bytes 589824 | tf_op jit(solution)/shard_map/all_to_all | solution.py:325
  31.8 0.1 copy.52
  31.9 0.1 fusion.3
  32.0 0.1 pad_maximum_fusion
  32.0 0.9 copy.41
  32.9 0.0 copy-start.5
  32.9 12.9 %all-to-all-start.1 = ((bf16[32,72,128]{2,1,0:T(8,128)(2,1)}), bf16[32,72,128]{2,1,0:T(8,128)(2,1)S(1)}, u32[]{:S(2)}, u32[]{:S(2)}) async-start(bf16[32,72,128]{2,1,0:T(8,128)(2,1)} %bitcast.9), calls=%async_computation.1 | async-start | bytes 1179648 | tf_op jit(solution)/shard_map/all_to_all | solution.py:328
  45.9 0.0 copy-done.5
  45.9 0.0 copy-start.3
  45.9 0.0 copy-start.4
  45.9 0.6 copy-done.3
  46.5 0.0 copy-done.4
  46.5 0.1 fusion.pick_ref
  46.6 11.5 %all-to-all-done.1 = bf16[32,72,128]{2,1,0:T(8,128)(2,1)S(1)} async-done(((bf16[32,72,128]{2,1,0:T(8,128)(2,1)}), bf16[32,72,128]{2,1,0:T(8,128)(2,1)S(1)}, u32[]{:S(2)}, u32[]{:S(2)}) %all-to-all-start.1) | async-done | bytes 589856 | tf_op jit(solution)/shard_map/all_to_all | solution.py:328
  58.1 0.1 copy.42
  58.3 0.1 copy.43
  58.4 0.1 broadcast_in_dim.6.code_ref
  58.4 0.2 pick.1
  58.7 0.0 collective-permute-start
  58.7 1.7 %collective-permute-start.1 = (bf16[6,32,128]{2,1,0:T(8,128)(2,1)S(1)}, bf16[6,32,128]{2,1,0:T(8,128)(2,1)S(1)}, u32[]{:S(2)}, u32[]{:S(2)}) collective-permute-start(bf16[6,32,128]{2,1,0:T(8,128)(2,1)S(1)} %get-tuple-element.12.center_ref), channel_id=1, source_target_pairs={{0,1},{1,2},{2,3},{3,4},{4,5},{5,6},{6,7},{7,0},{8,9},{9,10},{10,1... | collective-permute-start | bytes 147464 | tf_op jit(solution)/shard_map/ppermute | solution.py:335
  60.4 1.3 %collective-permute-start.2 = (bf16[3,32,128]{2,1,0:T(8,128)(2,1)S(1)}, bf16[3,32,128]{2,1,0:T(8,128)(2,1)S(1)}, u32[]{:S(2)}, u32[]{:S(2)}) collective-permute-start(bf16[3,32,128]{2,1,0:T(8,128)(2,1)S(1)} %get-tuple-element.13), channel_id=1, source_target_pairs={{128,0},{256,128},{384,256},{129,1},{257,129},{385,257},{130,2},{2... | collective-permute-start | bytes 73736 | tf_op jit(solution)/shard_map/ppermute | solution.py:336
  61.7 7.0 %collective-permute-start.3 = (bf16[3,32,128]{2,1,0:T(8,128)(2,1)S(1)}, bf16[3,32,128]{2,1,0:T(8,128)(2,1)S(1)}, u32[]{:S(2)}, u32[]{:S(2)}) collective-permute-start(bf16[3,32,128]{2,1,0:T(8,128)(2,1)S(1)} %get-tuple-element.13), channel_id=1, source_target_pairs={{0,128},{128,256},{256,384},{1,129},{129,257},{257,385},{2,130},{1... | collective-permute-start | bytes 73736 | tf_op jit(solution)/shard_map/ppermute | solution.py:337
  68.8 0.0 copy-start
  68.8 0.0 copy-start.1
  68.8 0.0 copy-start.2
  68.8 0.2 copy.44
  69.0 0.0 collective-permute-done.y_up_ref
  69.1 0.0 collective-permute-done.1.y_down_ref
  69.1 0.5 copy-done
  69.5 0.0 copy-done.1
  69.5 0.1 copy-done.2
  69.6 0.6 space.1.base_ref
  70.2 0.0 collective-permute-done.2.t_up_ref
  70.2 0.0 collective-permute-done.3.t_down_ref
  70.2 1.0 time.1
  71.2 12.2 %all_to_all.26 = f32[32,8,128]{2,1,0:T(8,128)S(1)} all-to-all(f32[32,8,128]{2,1,0:T(8,128)S(1)} %bitcast.68), channel_id=1, replica_groups=mesh['ta'=4,'zh'=4,'x'=4,'y'=4,'core'=2] {'x','y','core'}, dimensions={0} | all-to-all | bytes 262144 | tf_op jit(solution)/shard_map/all_to_all | solution.py:343
  83.5 17.3 %all_to_all.27 = f32[16,8,128]{2,1,0:T(8,128)S(1)} all-to-all(f32[16,8,128]{2,1,0:T(8,128)S(1)} %broadcast_in_dim.7), channel_id=1, replica_groups=mesh['ta'=4,'zh'=4,'x'=4,'y'=4,'core'=2] {'zh','x'}, dimensions={0} | all-to-all | bytes 131072 | tf_op jit(solution)/shard_map/all_to_all | solution.py:345
  100.8 9.5 %all_to_all.28 = f32[8,32,128]{2,1,0:T(8,128)S(1)} all-to-all(f32[8,32,128]{2,1,0:T(8,128)S(1)} %broadcast_in_dim.8), channel_id=1, replica_groups=mesh['ta'=4,'zh'=4,'x'=4,'y'=4,'core'=2] {'y','core'}, dimensions={0} | all-to-all | bytes 262144 | tf_op jit(solution)/shard_map/all_to_all | solution.py:349
  110.3 0.7 copy.54
  (17 shorter events, 0.3 us)
Async XLA Ops:
  32.9 12.9 %copy-start.5 = (s32[32]{0:T(128)S(1)}, s32[32]{0:T(128)}, u32[]{:S(2)}) copy-start(s32[32]{0:T(128)} %param.11) | copy-start | bytes 388
  32.9 25.2 %all-to-all-start.1 = ((bf16[32,72,128]{2,1,0:T(8,128)(2,1)}), bf16[32,72,128]{2,1,0:T(8,128)(2,1)S(1)}, u32[]{:S(2)}, u32[]{:S(2)}) async-start(bf16[32,72,128]{2,1,0:T(8,128)(2,1)} %bitcast.9), calls=%async_computation.1 | async-start | bytes 1179648 | tf_op jit(solution)/shard_map/all_to_all | solution.py:328
  45.9 0.7 copy-start.3
  45.9 0.7 copy-start.4
  58.7 10.4 %collective-permute-start = (bf16[6,32,128]{2,1,0:T(8,128)(2,1)S(1)}, bf16[6,32,128]{2,1,0:T(8,128)(2,1)S(1)}, u32[]{:S(2)}, u32[]{:S(2)}) collective-permute-start(bf16[6,32,128]{2,1,0:T(8,128)(2,1)S(1)} %get-tuple-element.12.center_ref), channel_id=1, source_target_pairs={{0,7},{1,0},{2,1},{3,2},{4,3},{5,4},{6,5},{7,6},{8,15},{9,8},{10,9... | collective-permute-start | bytes 147464 | tf_op jit(solution)/shard_map/ppermute | solution.py:334
  58.7 10.4 %collective-permute-start.1 = (bf16[6,32,128]{2,1,0:T(8,128)(2,1)S(1)}, bf16[6,32,128]{2,1,0:T(8,128)(2,1)S(1)}, u32[]{:S(2)}, u32[]{:S(2)}) collective-permute-start(bf16[6,32,128]{2,1,0:T(8,128)(2,1)S(1)} %get-tuple-element.12.center_ref), channel_id=1, source_target_pairs={{0,1},{1,2},{2,3},{3,4},{4,5},{5,6},{6,7},{7,0},{8,9},{9,10},{10,1... | collective-permute-start | bytes 147464 | tf_op jit(solution)/shard_map/ppermute | solution.py:335
  60.4 9.7 %collective-permute-start.2 = (bf16[3,32,128]{2,1,0:T(8,128)(2,1)S(1)}, bf16[3,32,128]{2,1,0:T(8,128)(2,1)S(1)}, u32[]{:S(2)}, u32[]{:S(2)}) collective-permute-start(bf16[3,32,128]{2,1,0:T(8,128)(2,1)S(1)} %get-tuple-element.13), channel_id=1, source_target_pairs={{128,0},{256,128},{384,256},{129,1},{257,129},{385,257},{130,2},{2... | collective-permute-start | bytes 73736 | tf_op jit(solution)/shard_map/ppermute | solution.py:336
  61.7 8.5 %collective-permute-start.3 = (bf16[3,32,128]{2,1,0:T(8,128)(2,1)S(1)}, bf16[3,32,128]{2,1,0:T(8,128)(2,1)S(1)}, u32[]{:S(2)}, u32[]{:S(2)}) collective-permute-start(bf16[3,32,128]{2,1,0:T(8,128)(2,1)S(1)} %get-tuple-element.13), channel_id=1, source_target_pairs={{0,128},{128,256},{256,384},{1,129},{129,257},{257,385},{2,130},{1... | collective-permute-start | bytes 73736 | tf_op jit(solution)/shard_map/ppermute | solution.py:337
  68.8 0.7 copy-start
  68.8 0.7 copy-start.1
  68.8 0.8 copy-start.2

commit v5 on v4

--- a/solution.py
+++ b/solution.py
@@ -27,9 +27,9 @@
         center_ref[k] = value.astype(jnp.bfloat16)
         used.append(jnp.where(match, value, pltpu.roll(value, 64, 1)))
     for colour in range(3):
-        halved_ref[colour] = jnp.where(lane < 64, used[2 * colour], used[2 * colour + 1]).astype(
-            jnp.bfloat16
-        )
+        halved = jnp.where(lane < 64, used[2 * colour], used[2 * colour + 1]).astype(jnp.bfloat16)
+        for slice_index in range(4):
+            halved_ref[slice_index, colour] = halved
 
 
 def colour_forward(ref, direction, real, imag):
@@ -243,7 +243,7 @@
         pick_kernel,
         out_shape=(
             jax.ShapeDtypeStruct((6, SOURCES, SITES), jnp.bfloat16),
-            jax.ShapeDtypeStruct((3, SOURCES, SITES), jnp.bfloat16),
+            jax.ShapeDtypeStruct((4, 3, SOURCES, SITES), jnp.bfloat16),
         ),
         compiler_params=pltpu.CompilerParams(vmem_limit_bytes=8 * 2**20),
         name="pick",
@@ -330,24 +330,23 @@
     vectors = pieces[:, :6].transpose(1, 0, 2, 3).reshape(6, EIGEN, SITES)
     others = pieces[:, 6:].transpose(1, 0, 2, 3).reshape(12, EIGEN, SITES)
     center, halved = pick_sources(pick, vectors, code)
-    halos = [
-        lax.ppermute(center, ("y", "core"), ring(8, -1)),
-        lax.ppermute(center, ("y", "core"), ring(8, 1)),
-        lax.ppermute(halved, "ta", ring(4, -1, False)),
-        lax.ppermute(halved, "ta", ring(4, 1, False)),
-    ]
+    y_up = lax.ppermute(center, ("y", "core"), ring(8, -1))
+    y_down = lax.ppermute(center, ("y", "core"), ring(8, 1))
+    times = lax.all_to_all(halved, "ta", split_axis=0, concat_axis=0, tiled=True)
+    t_up = lax.dynamic_index_in_dim(times, jnp.minimum(time + 1, 3), 0, keepdims=False)
+    t_down = lax.dynamic_index_in_dim(times, jnp.maximum(time - 1, 0), 0, keepdims=False)
+    halos = [y_up, y_down, t_up, t_down]
     base = space_part(others, pick, center, halos[0], halos[1], links, back, clover, code)
     propagated, sums = time_part(vectors, base, halos[2], halos[3], links, back, code)
     sums = sums.reshape(2, 32, 4, 128).transpose(0, 2, 1, 3)
-    parts = sums.reshape(8, 4, 8, 128).transpose(1, 0, 2, 3).reshape(32, 8, 128)
-    parts = lax.all_to_all(parts, DOMAIN, split_axis=0, concat_axis=0, tiled=True)
+    parts = lax.all_to_all(sums.reshape(32, 8, 128), DOMAIN, split_axis=0, concat_axis=0, tiled=True)
     part = jnp.sum(parts, axis=0)
     parts = lax.all_to_all(
-        jnp.broadcast_to(part[None], (16, 8, 128)), ("zh", "x"), split_axis=0, concat_axis=0, tiled=True
-    )
-    part = jnp.sum(parts.reshape(4, 32, 128), axis=0) * (1.0 / math.sqrt(3.0 * 64 * 16 * 16))
+        jnp.broadcast_to(part[None], (4, 8, 128)), "zh", split_axis=0, concat_axis=0, tiled=True
+    )
+    part = jnp.sum(parts, axis=0) * (1.0 / math.sqrt(3.0 * 64 * 16 * 16))
     whole = lax.all_to_all(
-        jnp.broadcast_to(part[None], (8, 32, 128)), ("y", "core"), split_axis=0, concat_axis=0, tiled=True
+        jnp.broadcast_to(part[None], (32, 8, 128)), DOMAIN, split_axis=0, concat_axis=0, tiled=True
     )
     return (
         propagated.reshape(SOURCES, 4, 3, 2, 1, 1, SITES),

time: 111 us -> 113 us (1.018)
  waiting for transfers between devices: 11.5 us -> 14.9 us
  starting transfers between devices: 23 us -> 19.7 us
  blocking collectives: 69 us -> 70.4 us
    ppermute x4 -> x2, starting transfers between devices: 10.1 us -> 0.51 us  [the longest x1 0.37 us: body(): y_down = lax.ppermute(center, ('y', 'core'), ring(8, 1))]
    all_to_all x0 -> x1, starting transfers between devices: none -> 6.25 us  [body(): lax.all_to_all(halved, 'ta', split_axis=0, concat_axis=0, tiled=True)]
    ppermute x4 -> x2, waiting for transfers between devices: 0.01 us -> 3.39 us  [the longest x1 2.63 us: body(): y_up = lax.ppermute(center, ('y', 'core'), ring(8, -1))]
    all_to_all x3, blocking collectives: 39 us -> 40.4 us  [the longest x1 14 us: body(): lax.all_to_all(jnp.broadcast_to(part[None], (4, 8, 128)), 'zh', split_axi...]
  transfers between devices with their start and end apart: 5 -> 4, of which waited for: 1 -> 3; matrix products, arithmetic and copies ran while one was open for 0% -> 0% of each run, Pallas kernels for 1% -> 0%
where the time goes in v5:
time: 113 us; the launch traced here: 112 us
  blocking collectives  70.4 us (62%)
  starting transfers between devices  19.7 us (17%)
  waiting for transfers between devices  14.9 us (13%)
  local copies, waits for them, and re-layouts  3.92 us (3%)
  Pallas kernels  2.43 us (2%)
    all_to_all x1, blocking collectives, body(): slabs = lax.all_to_all(slabs, 'zh', split_axis=0, concat_axis=0, tiled=True)  30 us
    all_to_all x1, blocking collectives, body(): lax.all_to_all(jnp.broadcast_to(part[None], (4, 8, 128)), 'zh', split_axi...  14 us
    all_to_all x1, blocking collectives, body(): lax.all_to_all(sums.reshape(32, 8, 128), DOMAIN, split_axis=0, concat_axi...  13.7 us
    all_to_all x1, starting transfers between devices, body(): lax.all_to_all(pieces, DOMAIN, split_axis=0, concat_axis=0, tiled=True)  12.9 us
    all_to_all x1, blocking collectives, body(): lax.all_to_all(jnp.broadcast_to(part[None], (32, 8, 128)), DOMAIN, split_...  12.7 us
    all_to_all x1, waiting for transfers between devices, body(): lax.all_to_all(pieces, DOMAIN, split_axis=0, concat_axis=0, tiled=True)  11.5 us
    all_to_all x1, starting transfers between devices, body(): lax.all_to_all(halved, 'ta', split_axis=0, concat_axis=0, tiled=True)  6.25 us
    ppermute x1, waiting for transfers between devices, body(): y_up = lax.ppermute(center, ('y', 'core'), ring(8, -1))  2.63 us
  transfers between devices with their start and end apart: 4, of which 3 were waited for; matrix products, arithmetic and copies ran while one was open for 0% of the time, Pallas kernels for 0%

profile of v5, /device:TPU:1, one launch (start us, length us, event | category | flops | bytes accessed | tf_op | source)
XLA Modules:
  0.0 112.5 jit_solution(4896158801529398051)
XLA Ops:
  0.6 1.0 copy.45
  1.8 30.0 %all_to_all.30 = bf16[4,6,6,8,128]{4,3,2,1,0:T(8,128)(2,1)S(1)} all-to-all(bf16[4,6,6,8,128]{4,3,2,1,0:T(8,128)(2,1)S(1)} %pad_maximum_fusion.1), channel_id=1, replica_groups=mesh['ta'=4,'zh'=4,'x'=4,'y'=4,'core'=2] {'zh'}, dimensions={0} | all-to-all | bytes 589824 | tf_op jit(solution)/shard_map/all_to_all | solution.py:325
  31.8 0.1 copy.48
  31.9 0.1 fusion.3
  32.0 0.1 pad_maximum_fusion
  32.0 0.9 copy.38
  32.9 0.0 copy-start.5
  32.9 12.9 %all-to-all-start.1 = ((bf16[32,72,128]{2,1,0:T(8,128)(2,1)}), bf16[32,72,128]{2,1,0:T(8,128)(2,1)S(1)}, u32[]{:S(2)}, u32[]{:S(2)}) async-start(bf16[32,72,128]{2,1,0:T(8,128)(2,1)} %bitcast.9), calls=%async_computation.1 | async-start | bytes 1179648 | tf_op jit(solution)/shard_map/all_to_all | solution.py:328
  45.9 0.0 copy-done.5
  45.9 0.0 copy-start.3
  45.9 0.0 copy-start.4
  45.9 0.6 copy-done.3
  46.5 0.0 copy-done.4
  46.6 0.1 fusion.pick_ref
  46.6 11.5 %all-to-all-done.1 = bf16[32,72,128]{2,1,0:T(8,128)(2,1)S(1)} async-done(((bf16[32,72,128]{2,1,0:T(8,128)(2,1)}), bf16[32,72,128]{2,1,0:T(8,128)(2,1)S(1)}, u32[]{:S(2)}, u32[]{:S(2)}) %all-to-all-start.1) | async-done | bytes 589856 | tf_op jit(solution)/shard_map/all_to_all | solution.py:328
  58.1 0.1 copy.39
  58.3 0.1 copy.40
  58.4 0.1 broadcast_in_dim.6.code_ref
  58.4 0.9 pick.1
  59.3 6.2 %all-to-all-start.2 = ((bf16[4,3,32,128]{3,2,1,0:T(8,128)(2,1)}), bf16[4,3,32,128]{3,2,1,0:T(8,128)(2,1)S(1)}, u32[]{:S(2)}, u32[]{:S(2)}) async-start(bf16[4,3,32,128]{3,2,1,0:T(8,128)(2,1)} %get-tuple-element.13), calls=%async_computation.2 | async-start | bytes 196608 | tf_op jit(solution)/shard_map/all_to_all | solution.py:335
  65.6 0.4 collective-permute-start.1
  65.9 0.1 collective-permute-start
  66.1 0.0 copy-start
  66.1 0.0 copy-start.1
  66.1 0.0 copy-start.2
  66.2 0.2 copy.41
  66.4 0.8 collective-permute-done.1.y_down_ref
  67.1 2.6 %collective-permute-done.y_up_ref = bf16[6,32,128]{2,1,0:T(8,128)(2,1)S(1)} collective-permute-done((bf16[6,32,128]{2,1,0:T(8,128)(2,1)S(1)}, bf16[6,32,128]{2,1,0:T(8,128)(2,1)S(1)}, u32[]{:S(2)}, u32[]{:S(2)}) %collective-permute-start) | collective-permute-done | bytes 49184 | tf_op jit(solution)/shard_map/ppermute | solution.py:333
  69.8 0.0 copy-done
  69.8 0.0 copy-done.1
  69.8 0.0 copy-done.2
  69.8 0.6 space.1.base_ref
  70.3 0.0 all-to-all-done.2
  70.4 1.0 time.1
  71.4 13.7 %all_to_all.31 = f32[32,8,128]{2,1,0:T(8,128)S(1)} all-to-all(f32[32,8,128]{2,1,0:T(8,128)S(1)} %bitcast.65), channel_id=1, replica_groups=mesh['ta'=4,'zh'=4,'x'=4,'y'=4,'core'=2] {'x','y','core'}, dimensions={0} | all-to-all | bytes 262144 | tf_op jit(solution)/shard_map/all_to_all | solution.py:342
  85.1 14.0 %all_to_all.32 = f32[4,8,128]{2,1,0:T(8,128)S(1)} all-to-all(f32[4,8,128]{2,1,0:T(8,128)S(1)} %broadcast_in_dim.7), channel_id=1, replica_groups=mesh['ta'=4,'zh'=4,'x'=4,'y'=4,'core'=2] {'zh'}, dimensions={0} | all-to-all | bytes 32768 | tf_op jit(solution)/shard_map/all_to_all | solution.py:344
  99.1 12.7 %all_to_all.33 = f32[32,8,128]{2,1,0:T(8,128)S(1)} all-to-all(f32[32,8,128]{2,1,0:T(8,128)S(1)} %broadcast_in_dim.8), channel_id=1, replica_groups=mesh['ta'=4,'zh'=4,'x'=4,'y'=4,'core'=2] {'x','y','core'}, dimensions={0} | all-to-all | bytes 262144 | tf_op jit(solution)/shard_map/all_to_all | solution.py:348
  111.8 0.7 copy.50
  (17 shorter events, 0.3 us)
Async XLA Ops:
  32.9 12.9 %copy-start.5 = (s32[32]{0:T(128)S(1)}, s32[32]{0:T(128)}, u32[]{:S(2)}) copy-start(s32[32]{0:T(128)} %param.11) | copy-start | bytes 388
  32.9 25.2 %all-to-all-start.1 = ((bf16[32,72,128]{2,1,0:T(8,128)(2,1)}), bf16[32,72,128]{2,1,0:T(8,128)(2,1)S(1)}, u32[]{:S(2)}, u32[]{:S(2)}) async-start(bf16[32,72,128]{2,1,0:T(8,128)(2,1)} %bitcast.9), calls=%async_computation.1 | async-start | bytes 1179648 | tf_op jit(solution)/shard_map/all_to_all | solution.py:328
  45.9 0.7 copy-start.3
  45.9 0.7 copy-start.4
  59.3 11.0 %all-to-all-start.2 = ((bf16[4,3,32,128]{3,2,1,0:T(8,128)(2,1)}), bf16[4,3,32,128]{3,2,1,0:T(8,128)(2,1)S(1)}, u32[]{:S(2)}, u32[]{:S(2)}) async-start(bf16[4,3,32,128]{3,2,1,0:T(8,128)(2,1)} %get-tuple-element.13), calls=%async_computation.2 | async-start | bytes 196608 | tf_op jit(solution)/shard_map/all_to_all | solution.py:335
  65.6 1.5 %collective-permute-start.1 = (bf16[6,32,128]{2,1,0:T(8,128)(2,1)S(1)}, bf16[6,32,128]{2,1,0:T(8,128)(2,1)S(1)}, u32[]{:S(2)}, u32[]{:S(2)}) collective-permute-start(bf16[6,32,128]{2,1,0:T(8,128)(2,1)S(1)} %get-tuple-element.12.center_ref), channel_id=1, source_target_pairs={{0,1},{1,2},{2,3},{3,4},{4,5},{5,6},{6,7},{7,0},{8,9},{9,10},{10,1... | collective-permute-start | bytes 147464 | tf_op jit(solution)/shard_map/ppermute | solution.py:334
  65.9 3.8 %collective-permute-start = (bf16[6,32,128]{2,1,0:T(8,128)(2,1)S(1)}, bf16[6,32,128]{2,1,0:T(8,128)(2,1)S(1)}, u32[]{:S(2)}, u32[]{:S(2)}) collective-permute-start(bf16[6,32,128]{2,1,0:T(8,128)(2,1)S(1)} %get-tuple-element.12.center_ref), channel_id=1, source_target_pairs={{0,7},{1,0},{2,1},{3,2},{4,3},{5,4},{6,5},{7,6},{8,15},{9,8},{10,9... | collective-permute-start | bytes 147464 | tf_op jit(solution)/shard_map/ppermute | solution.py:333
  66.1 3.6 %copy-start = (bf16[4,3,3,2,1,1,128]{6,3,5,4,2,1,0:T(2,128)(2,1)S(1)}, bf16[4,3,3,2,1,1,128]{6,3,5,4,2,1,0:T(2,128)(2,1)}, u32[]{:S(2)}) copy-start(bf16[4,3,3,2,1,1,128]{6,3,5,4,2,1,0:T(2,128)(2,1)} %param.8) | copy-start | bytes 55300
  66.1 3.6 %copy-start.1 = (bf16[4,3,3,2,1,1,128]{6,3,5,4,2,1,0:T(2,128)(2,1)S(1)}, bf16[4,3,3,2,1,1,128]{6,3,5,4,2,1,0:T(2,128)(2,1)}, u32[]{:S(2)}) copy-start(bf16[4,3,3,2,1,1,128]{6,3,5,4,2,1,0:T(2,128)(2,1)} %param.9) | copy-start | bytes 55300
  66.1 3.6 %copy-start.2 = (bf16[2,6,6,2,1,1,128]{6,3,5,4,2,1,0:T(2,128)(2,1)S(1)}, bf16[2,6,6,2,1,1,128]{6,3,5,4,2,1,0:T(2,128)(2,1)}, u32[]{:S(2)}) copy-start(bf16[2,6,6,2,1,1,128]{6,3,5,4,2,1,0:T(2,128)(2,1)} %param.10) | copy-start | bytes 110596

commit v6 on v4

--- a/solution.py
+++ b/solution.py
@@ -339,15 +339,14 @@
     base = space_part(others, pick, center, halos[0], halos[1], links, back, clover, code)
     propagated, sums = time_part(vectors, base, halos[2], halos[3], links, back, code)
     sums = sums.reshape(2, 32, 4, 128).transpose(0, 2, 1, 3)
-    parts = sums.reshape(8, 4, 8, 128).transpose(1, 0, 2, 3).reshape(32, 8, 128)
-    parts = lax.all_to_all(parts, DOMAIN, split_axis=0, concat_axis=0, tiled=True)
+    parts = lax.all_to_all(sums.reshape(32, 8, 128), DOMAIN, split_axis=0, concat_axis=0, tiled=True)
     part = jnp.sum(parts, axis=0)
     parts = lax.all_to_all(
-        jnp.broadcast_to(part[None], (16, 8, 128)), ("zh", "x"), split_axis=0, concat_axis=0, tiled=True
-    )
-    part = jnp.sum(parts.reshape(4, 32, 128), axis=0) * (1.0 / math.sqrt(3.0 * 64 * 16 * 16))
+        jnp.broadcast_to(part[None], (4, 8, 128)), "zh", split_axis=0, concat_axis=0, tiled=True
+    )
+    part = jnp.sum(parts, axis=0) * (1.0 / math.sqrt(3.0 * 64 * 16 * 16))
     whole = lax.all_to_all(
-        jnp.broadcast_to(part[None], (8, 32, 128)), ("y", "core"), split_axis=0, concat_axis=0, tiled=True
+        jnp.broadcast_to(part[None], (32, 8, 128)), DOMAIN, split_axis=0, concat_axis=0, tiled=True
     )
     return (
         propagated.reshape(SOURCES, 4, 3, 2, 1, 1, SITES),

time: 111 us -> 111 us (level)
  no operation moved by 1% of the time
where the time goes in v6:
time: 111 us
  blocking collectives  69.1 us (62%)
  starting transfers between devices  23 us (21%)
  waiting for transfers between devices  11.5 us (10%)
  local copies, waits for them, and re-layouts  4.44 us (4%)
  Pallas kernels  1.78 us (2%)
    all_to_all x1, blocking collectives, body(): slabs = lax.all_to_all(slabs, 'zh', split_axis=0, concat_axis=0, tiled=True)  30 us
    all_to_all x1, blocking collectives, body(): lax.all_to_all(jnp.broadcast_to(part[None], (4, 8, 128)), 'zh', split_axi...  14.2 us
    all_to_all x1, starting transfers between devices, body(): lax.all_to_all(pieces, DOMAIN, split_axis=0, concat_axis=0, tiled=True)  12.9 us
    all_to_all x1, blocking collectives, body(): lax.all_to_all(jnp.broadcast_to(part[None], (32, 8, 128)), DOMAIN, split_...  12.6 us
    all_to_all x1, blocking collectives, body(): lax.all_to_all(sums.reshape(32, 8, 128), DOMAIN, split_axis=0, concat_axi...  12.2 us
    all_to_all x1, waiting for transfers between devices, body(): lax.all_to_all(pieces, DOMAIN, split_axis=0, concat_axis=0, tiled=True)  11.5 us
    ppermute x1, starting transfers between devices, body(): lax.ppermute(halved, 'ta', ring(4, 1, False))  7.03 us
    unnamed x14, local copies, waits for them, and re-layouts  2.8 us
  transfers between devices with their start and end apart: 5, of which 1 were waited for; matrix products, arithmetic and copies ran while one was open for 0% of the time, Pallas kernels for 1%

profile of v6, /device:TPU:1, one launch (start us, length us, event | category | flops | bytes accessed | tf_op | source)
XLA Modules:
  0.0 111.0 jit_solution(11832539665068814655)
XLA Ops:
  0.6 1.0 copy.45
  1.8 30.0 %all_to_all.25 = bf16[4,6,6,8,128]{4,3,2,1,0:T(8,128)(2,1)S(1)} all-to-all(bf16[4,6,6,8,128]{4,3,2,1,0:T(8,128)(2,1)S(1)} %pad_maximum_fusion.1), channel_id=1, replica_groups=mesh['ta'=4,'zh'=4,'x'=4,'y'=4,'core'=2] {'zh'}, dimensions={0} | all-to-all | bytes 589824 | tf_op jit(solution)/shard_map/all_to_all | solution.py:325
  31.8 0.1 copy.48
  31.9 0.1 fusion.3
  32.0 0.1 pad_maximum_fusion
  32.0 0.9 copy.38
  32.9 0.0 copy-start.5
  32.9 12.9 %all-to-all-start.1 = ((bf16[32,72,128]{2,1,0:T(8,128)(2,1)}), bf16[32,72,128]{2,1,0:T(8,128)(2,1)S(1)}, u32[]{:S(2)}, u32[]{:S(2)}) async-start(bf16[32,72,128]{2,1,0:T(8,128)(2,1)} %bitcast.9), calls=%async_computation.1 | async-start | bytes 1179648 | tf_op jit(solution)/shard_map/all_to_all | solution.py:328
  45.9 0.0 copy-done.5
  45.9 0.0 copy-start.3
  45.9 0.0 copy-start.4
  45.9 0.6 copy-done.3
  46.5 0.0 copy-done.4
  46.5 0.1 fusion.pick_ref
  46.6 11.5 %all-to-all-done.1 = bf16[32,72,128]{2,1,0:T(8,128)(2,1)S(1)} async-done(((bf16[32,72,128]{2,1,0:T(8,128)(2,1)}), bf16[32,72,128]{2,1,0:T(8,128)(2,1)S(1)}, u32[]{:S(2)}, u32[]{:S(2)}) %all-to-all-start.1) | async-done | bytes 589856 | tf_op jit(solution)/shard_map/all_to_all | solution.py:328
  58.1 0.1 copy.39
  58.3 0.1 copy.40
  58.4 0.1 broadcast_in_dim.6.code_ref
  58.4 0.2 pick.1
  58.7 0.0 collective-permute-start
  58.7 1.7 %collective-permute-start.1 = (bf16[6,32,128]{2,1,0:T(8,128)(2,1)S(1)}, bf16[6,32,128]{2,1,0:T(8,128)(2,1)S(1)}, u32[]{:S(2)}, u32[]{:S(2)}) collective-permute-start(bf16[6,32,128]{2,1,0:T(8,128)(2,1)S(1)} %get-tuple-element.12.center_ref), channel_id=1, source_target_pairs={{0,1},{1,2},{2,3},{3,4},{4,5},{5,6},{6,7},{7,0},{8,9},{9,10},{10,1... | collective-permute-start | bytes 147464 | tf_op jit(solution)/shard_map/ppermute | solution.py:335
  60.4 1.3 %collective-permute-start.2 = (bf16[3,32,128]{2,1,0:T(8,128)(2,1)S(1)}, bf16[3,32,128]{2,1,0:T(8,128)(2,1)S(1)}, u32[]{:S(2)}, u32[]{:S(2)}) collective-permute-start(bf16[3,32,128]{2,1,0:T(8,128)(2,1)S(1)} %get-tuple-element.13), channel_id=1, source_target_pairs={{128,0},{256,128},{384,256},{129,1},{257,129},{385,257},{130,2},{2... | collective-permute-start | bytes 73736 | tf_op jit(solution)/shard_map/ppermute | solution.py:336
  61.7 7.0 %collective-permute-start.3 = (bf16[3,32,128]{2,1,0:T(8,128)(2,1)S(1)}, bf16[3,32,128]{2,1,0:T(8,128)(2,1)S(1)}, u32[]{:S(2)}, u32[]{:S(2)}) collective-permute-start(bf16[3,32,128]{2,1,0:T(8,128)(2,1)S(1)} %get-tuple-element.13), channel_id=1, source_target_pairs={{0,128},{128,256},{256,384},{1,129},{129,257},{257,385},{2,130},{1... | collective-permute-start | bytes 73736 | tf_op jit(solution)/shard_map/ppermute | solution.py:337
  68.8 0.0 copy-start
  68.8 0.0 copy-start.1
  68.8 0.0 copy-start.2
  68.8 0.2 copy.41
  69.0 0.0 collective-permute-done.y_up_ref
  69.1 0.0 collective-permute-done.1.y_down_ref
  69.1 0.5 copy-done
  69.5 0.0 copy-done.1
  69.5 0.1 copy-done.2
  69.6 0.6 space.1.base_ref
  70.2 0.0 collective-permute-done.2.t_up_ref
  70.2 0.0 collective-permute-done.3.t_down_ref
  70.2 1.0 time.1
  71.2 12.2 %all_to_all.26 = f32[32,8,128]{2,1,0:T(8,128)S(1)} all-to-all(f32[32,8,128]{2,1,0:T(8,128)S(1)} %bitcast.61), channel_id=1, replica_groups=mesh['ta'=4,'zh'=4,'x'=4,'y'=4,'core'=2] {'x','y','core'}, dimensions={0} | all-to-all | bytes 262144 | tf_op jit(solution)/shard_map/all_to_all | solution.py:342
  83.4 14.2 %all_to_all.27 = f32[4,8,128]{2,1,0:T(8,128)S(1)} all-to-all(f32[4,8,128]{2,1,0:T(8,128)S(1)} %broadcast_in_dim.7), channel_id=1, replica_groups=mesh['ta'=4,'zh'=4,'x'=4,'y'=4,'core'=2] {'zh'}, dimensions={0} | all-to-all | bytes 32768 | tf_op jit(solution)/shard_map/all_to_all | solution.py:344
  97.7 12.6 %all_to_all.28 = f32[32,8,128]{2,1,0:T(8,128)S(1)} all-to-all(f32[32,8,128]{2,1,0:T(8,128)S(1)} %broadcast_in_dim.8), channel_id=1, replica_groups=mesh['ta'=4,'zh'=4,'x'=4,'y'=4,'core'=2] {'x','y','core'}, dimensions={0} | all-to-all | bytes 262144 | tf_op jit(solution)/shard_map/all_to_all | solution.py:348
  110.3 0.7 copy.50
  (16 shorter events, 0.3 us)
Async XLA Ops:
  32.9 12.9 %copy-start.5 = (s32[32]{0:T(128)S(1)}, s32[32]{0:T(128)}, u32[]{:S(2)}) copy-start(s32[32]{0:T(128)} %param.11) | copy-start | bytes 388
  32.9 25.2 %all-to-all-start.1 = ((bf16[32,72,128]{2,1,0:T(8,128)(2,1)}), bf16[32,72,128]{2,1,0:T(8,128)(2,1)S(1)}, u32[]{:S(2)}, u32[]{:S(2)}) async-start(bf16[32,72,128]{2,1,0:T(8,128)(2,1)} %bitcast.9), calls=%async_computation.1 | async-start | bytes 1179648 | tf_op jit(solution)/shard_map/all_to_all | solution.py:328
  45.9 0.7 copy-start.3
  45.9 0.7 copy-start.4
  58.7 10.4 %collective-permute-start = (bf16[6,32,128]{2,1,0:T(8,128)(2,1)S(1)}, bf16[6,32,128]{2,1,0:T(8,128)(2,1)S(1)}, u32[]{:S(2)}, u32[]{:S(2)}) collective-permute-start(bf16[6,32,128]{2,1,0:T(8,128)(2,1)S(1)} %get-tuple-element.12.center_ref), channel_id=1, source_target_pairs={{0,7},{1,0},{2,1},{3,2},{4,3},{5,4},{6,5},{7,6},{8,15},{9,8},{10,9... | collective-permute-start | bytes 147464 | tf_op jit(solution)/shard_map/ppermute | solution.py:334
  58.7 10.4 %collective-permute-start.1 = (bf16[6,32,128]{2,1,0:T(8,128)(2,1)S(1)}, bf16[6,32,128]{2,1,0:T(8,128)(2,1)S(1)}, u32[]{:S(2)}, u32[]{:S(2)}) collective-permute-start(bf16[6,32,128]{2,1,0:T(8,128)(2,1)S(1)} %get-tuple-element.12.center_ref), channel_id=1, source_target_pairs={{0,1},{1,2},{2,3},{3,4},{4,5},{5,6},{6,7},{7,0},{8,9},{9,10},{10,1... | collective-permute-start | bytes 147464 | tf_op jit(solution)/shard_map/ppermute | solution.py:335
  60.4 9.7 %collective-permute-start.2 = (bf16[3,32,128]{2,1,0:T(8,128)(2,1)S(1)}, bf16[3,32,128]{2,1,0:T(8,128)(2,1)S(1)}, u32[]{:S(2)}, u32[]{:S(2)}) collective-permute-start(bf16[3,32,128]{2,1,0:T(8,128)(2,1)S(1)} %get-tuple-element.13), channel_id=1, source_target_pairs={{128,0},{256,128},{384,256},{129,1},{257,129},{385,257},{130,2},{2... | collective-permute-start | bytes 73736 | tf_op jit(solution)/shard_map/ppermute | solution.py:336
  61.7 8.5 %collective-permute-start.3 = (bf16[3,32,128]{2,1,0:T(8,128)(2,1)S(1)}, bf16[3,32,128]{2,1,0:T(8,128)(2,1)S(1)}, u32[]{:S(2)}, u32[]{:S(2)}) collective-permute-start(bf16[3,32,128]{2,1,0:T(8,128)(2,1)S(1)} %get-tuple-element.13), channel_id=1, source_target_pairs={{0,128},{128,256},{256,384},{1,129},{129,257},{257,385},{2,130},{1... | collective-permute-start | bytes 73736 | tf_op jit(solution)/shard_map/ppermute | solution.py:337
  68.8 0.7 copy-start
  68.8 0.7 copy-start.1
  68.8 0.8 copy-start.2
